TPU v7x, 32 devices: a whole 2x2x4 slice. The times are simulated.
32 devices in a mesh: pipe: 2 (over y), ctx: 4 (over x, core), tp: 4 (over z).
Axes of the slice: x: 2, y: 2, z: 4, core: 2. Of those that a mesh axis runs over, the one named last changes fastest.
Arguments:
- x_in: bfloat16 [2, 512, 8192], P(None, 'ctx', 'tp'), may hold values from -6 to 6
- hidden_in: bfloat16 [2, 512, 8192], P(None, ('ctx', 'tp')), may hold values from -6 to 6
- gate_z: bfloat16 [2, 2, 512, 8192], P('pipe', None, 'ctx', 'tp'), may hold values from -6 to 6
- out_proj: bfloat16 [8192, 8192], P('tp', 'ctx'), may hold values from -0.0625 to 0.0625
- in_proj: bfloat16 [8192, 8192], P('tp', 'ctx'), may hold values from -0.0625 to 0.0625
- norm_gain: float32 [8192], replicated, may hold values from 0.1 to 1.9
- conv_weight: float32 [2, 4, 8192], P('pipe', None, 'tp'), may hold values from -3 to 3
- conv_bias: float32 [2, 8192], P('pipe', 'tp'), may hold values from -3 to 3
- x_proj: bfloat16 [2, 8192, 544], P('pipe', 'tp'), may hold values from -0.0625 to 0.0625
- dt_proj: bfloat16 [2, 512, 8192], P('pipe', None, 'tp'), may hold values from -0.25 to 0.25
- dt_bias: float32 [2, 8192], P('pipe', 'tp'), may hold values from -3 to -1
- decay_rate: float32 [2, 16, 8192], P('pipe', None, 'tp'), may hold values from 0.001953125 to 1
- skip: float32 [2, 8192], P('pipe', 'tp'), may hold values from 0.1 to 1.9
Outputs:
- mixed: bfloat16 [2, 2, 512, 8192], P('pipe', None, 'ctx', 'tp')
All inputs are finite; a program needn't handle non-finite values.
Results may differ from a plain program's by a relative error of at most 0.017.
Values may be sent and summed in bfloat16 or wider, within the bound.
A program may use at most 128 MiB of HBM per device.

v0:
```python
import jax
import jax.numpy as jnp
from jax import lax
from jax.sharding import PartitionSpec as P


def shifted(block, axis, distance):
    devices = range(lax.axis_size(axis))
    route = [(i - distance, i) for i in devices if i - distance in devices]
    return lax.ppermute(block, axis, route)


def entering(part, axis, combine, identity):
    place = lax.axis_index(axis)
    gathered = jax.tree.map(lambda a: lax.all_gather(a, axis), part)
    state = jax.tree.map(lambda a, e: jnp.zeros_like(a) + jnp.asarray(e, a.dtype), part, identity)

    def one(step, state):
        return combine(
            state, jax.tree.map(lambda a: lax.dynamic_index_in_dim(a, step, 0, False), gathered)
        )

    return lax.fori_loop(0, place, one, state)


def link_pair(earlier, later):
    return (earlier[0] * later[0], earlier[1] * later[0] + later[1])


def rank_norm(rate_low):
    return (
        rate_low * lax.rsqrt(jnp.mean(rate_low * rate_low, axis=1, keepdims=True) + 1e-06)
    ).astype(jnp.bfloat16)


def sweep_state(start_state, step_size, active_wide, input_map, output_map, decay):
    count = step_size.shape[0]
    span = 8
    blocks = count // span

    def fold_block(state, rows):
        step_rows, act_rows, in_rows, out_rows = rows
        outputs = []
        for inner in range(span):
            state = (
                jnp.exp(-step_rows[inner][None, :] * decay) * state
                + in_rows[inner][:, None] * (step_rows[inner] * act_rows[inner])[None, :]
            )
            outputs.append(jnp.sum(out_rows[inner][:, None] * state, axis=0))
        return (state, jnp.stack(outputs, axis=0))

    rows = (
        step_size.reshape(blocks, span, -1),
        active_wide.reshape(blocks, span, -1),
        input_map.reshape(blocks, span, -1),
        output_map.reshape(blocks, span, -1),
    )
    final_state, outputs = lax.scan(fold_block, start_state, rows)
    return (final_state, outputs.reshape(count, -1))


def run_section(inputs, gate, conv_weight, conv_bias, x_proj, dt_proj, dt_bias, decay_rate, skip):
    count = inputs.shape[0]
    width = inputs.shape[1]
    taps_count = conv_weight.shape[1]
    rank = dt_proj.shape[1]
    nstate = decay_rate.shape[1]
    rim_rows = shifted(inputs[count - (taps_count - 1) :], "ctx", 1)
    wide_in = inputs.astype(jnp.float32)
    padded = jnp.concatenate([rim_rows.astype(jnp.float32), wide_in], axis=0)
    convolved = conv_bias[0][None, :] + jnp.zeros((count, width), jnp.float32)
    for offset in range(taps_count):
        convolved = convolved + conv_weight[0, offset][None, :] * padded[offset : offset + count]
    activated = jax.nn.silu(convolved).astype(jnp.bfloat16)
    partial_proj = jnp.dot(activated, x_proj[0], preferred_element_type=jnp.float32)
    projected = lax.psum(partial_proj, "tp")
    rate_normed = rank_norm(projected[:, :rank])
    maps = projected[:, rank:]
    step_size = jax.nn.softplus(
        jnp.dot(rate_normed, dt_proj[0], preferred_element_type=jnp.float32) + dt_bias[0][None, :]
    )
    input_map = maps[:, :nstate]
    output_map = maps[:, nstate:]
    active_wide = activated.astype(jnp.float32)
    decay = decay_rate[0]
    empty_state = jnp.zeros((nstate, width), jnp.float32)
    end_state, _ = sweep_state(empty_state, step_size, active_wide, input_map, output_map, decay)
    total_decay = jnp.exp(-decay * jnp.sum(step_size, axis=0)[None, :])
    _, incoming = entering(
        (total_decay, end_state),
        "ctx",
        link_pair,
        (jnp.ones_like(total_decay), jnp.zeros_like(end_state)),
    )
    _, state_response = sweep_state(incoming, step_size, active_wide, input_map, output_map, decay)
    response = state_response + skip[0][None, :] * active_wide
    return (response * jax.nn.silu(gate.astype(jnp.float32))).astype(jnp.bfloat16)


def shards(
    x_in,
    hidden_in,
    gate_z,
    out_proj,
    in_proj,
    norm_gain,
    conv_weight,
    conv_bias,
    x_proj,
    dt_proj,
    dt_bias,
    decay_rate,
    skip,
):
    micro = x_in.shape[0]
    segments = lax.axis_size("pipe")
    segment = lax.axis_index("pipe")
    ticks = micro + segments - 1
    own_link = jnp.where(segment == 0, out_proj, in_proj)
    link_full = lax.all_gather(own_link, "ctx", axis=1, tiled=True)
    results = jnp.zeros(gate_z.shape, jnp.bfloat16)
    received = jnp.zeros(hidden_in.shape[1:], jnp.bfloat16)
    for tick in range(ticks):
        own_rows = x_in[min(tick, micro - 1)]
        if tick == 0:
            inputs = own_rows
        else:
            wide = received.astype(jnp.float32)
            normed_share = (
                wide
                * lax.rsqrt(jnp.mean(wide * wide, axis=1, keepdims=True) + 1e-05)
                * norm_gain[None, :]
            ).astype(jnp.bfloat16)
            normed = lax.all_gather(normed_share, "tp", axis=0, tiled=True)
            from_link = lax.dot_general(
                normed, link_full, (((1,), (1,)), ((), ())), preferred_element_type=jnp.float32
            ).astype(jnp.bfloat16)
            inputs = jnp.where(segment == 0, own_rows, from_link)
        slot = tick - segment
        valid = jnp.logical_and(slot >= 0, slot < micro)
        safe_slot = jnp.clip(slot, 0, micro - 1)
        gate = lax.dynamic_index_in_dim(gate_z[0], safe_slot, 0, keepdims=False)
        mixed = run_section(
            inputs, gate, conv_weight, conv_bias, x_proj, dt_proj, dt_bias, decay_rate, skip
        )
        current = lax.dynamic_index_in_dim(results[0], safe_slot, 0, keepdims=False)
        chosen = jnp.where(valid, mixed, current)
        zero_index = jnp.zeros((), jnp.int32)
        results = lax.dynamic_update_slice(
            results, chosen[None, None], (zero_index, safe_slot, zero_index, zero_index)
        )
        if tick + 1 < ticks:
            partial_link = jnp.dot(mixed, link_full, preferred_element_type=jnp.float32)
            link_share = lax.psum_scatter(partial_link, "tp", scatter_dimension=0, tiled=True)
            carried = (hidden_in[min(tick, micro - 1)].astype(jnp.float32) + link_share).astype(
                jnp.bfloat16
            )
            received = shifted(carried, "pipe", 1)
    return results


def solution(mesh):
    in_specs = (
        P(None, "ctx", "tp"),
        P(None, ("ctx", "tp"), None),
        P("pipe", None, "ctx", "tp"),
        P("tp", "ctx"),
        P("tp", "ctx"),
        P(),
        P("pipe", None, "tp"),
        P("pipe", "tp"),
        P("pipe", "tp", None),
        P("pipe", None, "tp"),
        P("pipe", "tp"),
        P("pipe", None, "tp"),
        P("pipe", "tp"),
    )
    out_specs = P("pipe", None, "ctx", "tp")
    return jax.shard_map(shards, mesh=mesh, in_specs=in_specs, out_specs=out_specs, check_vma=False)
```

profile of v0, /device:TPU:11, one launch (start us, length us, event | category | flops | bytes accessed | tf_op | source)
XLA Modules:
  0.0 925.7 jit_solution(7755577693960524480)
XLA Ops:
  25.8 29.2 %all-reduce.4.cloned.1.call-done = f32[128,544]{0,1:T(8,128)} async-done(((f32[128,544]{0,1:T(8,128)}), f32[128,544]{0,1:T(8,128)}) %all-reduce.4.cloned.1.call-update) | async-done | bytes 278544 | tf_op jit(solution)/shard_map/psum | solution.py:76
  62.0 33.2 %while.111 = (s32[]{:T(128)}, f32[16,2048]{1,0:T(8,128)S(1)}, f32[16,8,2048]{2,1,0:T(8,128)}, f32[16,2048]{1,0:T(8,128)S(1)}, f32[16,8,16]{2,1,0:T(8,128)S(1)}, ...) while((s32[]{:T(128)}, f32[16,2048]{1,0:T(8,128)S(1)}, ...), condition=%wide.region_4.5_spmd.clone, body=%wide.region_3.4_spmd.clone.sunk | while | flops 1114122 | bytes 789263 | solution.py:58
  95.8 11.7 %all-gather = f32[64,2048]{1,0:T(8,128)S(1)} all-gather(f32[16,2048]{1,0:T(8,128)S(1)} %get-tuple-element.359), channel_id=2, replica_groups=mesh['pipe'=2,'ctx'=4,'tp'=4] {'ctx'}, dimensions={0}, use_global_device_ids=true | all-gather | bytes 655360 | tf_op jit(solution)/shard_map/all_gather | solution.py:15
  108.2 10.9 %all_gather.39 = f32[4,16,2048]{2,1,0:T(8,128)} all-gather(f32[1,16,2048]{2,1,0:T(8,128)S(1)} %multiply_exponential_fusion.2), channel_id=1, replica_groups=mesh['pipe'=2,'ctx'=4,'tp'=4] {'ctx'}, dimensions={0}, use_global_device_ids=true | all-gather | bytes 655360 | tf_op jit(solution)/shard_map/all_gather | solution.py:15
  123.3 62.7 %while.106 = (s32[]{:T(128)}, f32[16,2048]{1,0:T(8,128)S(1)}, f32[16,8,2048]{2,1,0:T(8,128)}, f32[16,8,2048]{2,1,0:T(8,128)}, f32[16,2048]{1,0:T(8,128)S(1)}, /*...) while((s32[]{:T(128)}, f32[16,2048]{1,0:T(8,128)S(1)}, ...), condition=%wide.region_16.17_spmd, body=%wide.region_7.16_spmd.sunk | while | flops 2375689 | bytes 1874069 | solution.py:58
  189.8 44.6 %all-gather.7.cloned.1.call-done = bf16[2048,8192]{1,0:T(8,128)(2,1)} async-done(((bf16[2048,2048]{1,0:T(8,128)(2,1)}), bf16[2048,8192]{1,0:T(8,128)(2,1)}) %all-gather.7.cloned.1.call-update) | async-done | bytes 33554448 | tf_op jit(solution)/shard_map/all_gather | solution.py:120
  234.4 17.1 %fusion.177 = f32[128,8192]{1,0:T(8,128)} fusion(bf16[128,2048]{1,0:T(8,128)(2,1)S(1)} %get-tuple-element.624, bf16[2048,8192]{1,0:T(8,128)(2,1)} %all-gather.7.cloned.1.call-done), kind=kOutput, calls=%fused_computation.474 | convolution fusion | flops 4294967296 | bytes 38273024 | tf_op jit(solution)/shard_map/dot_general | solution.py:153
  251.6 77.4 %reduce-scatter.3.cloned.1.call-done = f32[32,8192]{1,0:T(8,128)} async-done(((f32[128,8192]{1,0:T(8,128)}), f32[32,8192]{1,0:T(8,128)}) %reduce-scatter.3.cloned.1.call-update) | async-done | bytes 1048592 | tf_op jit(solution)/shard_map/reduce_scatter | solution.py:154
  333.6 10.6 %collective-permute-done.1 = bf16[32,8192]{1,0:T(8,128)(2,1)S(1)} collective-permute-done((bf16[32,8192]{1,0:T(8,128)(2,1)S(1)}, bf16[32,8192]{1,0:T(8,128)(2,1)S(1)}, u32[]{:S(2)}, u32[]{:S(2)}) %collective-permute-start.1) | collective-permute-done | bytes 524320 | tf_op jit(solution)/shard_map/ppermute | solution.py:10
  345.7 46.3 %all-gather.9.cloned.1.call-done = bf16[128,8192]{1,0:T(8,128)(2,1)} async-done(((bf16[32,8192]{1,0:T(8,128)(2,1)}), bf16[128,8192]{1,0:T(8,128)(2,1)}) %all-gather.9.cloned.1.call-update) | async-done | bytes 2097168 | tf_op jit(solution)/shard_map/all_gather | solution.py:134
  392.0 16.3 %fusion.173 = (f32[128,2048]{1,0:T(8,128)S(1)}, bf16[128,2048]{1,0:T(8,128)(2,1)S(1)}) fusion(bf16[128,8192]{1,0:T(8,128)(2,1)} %all-gather.9.cloned.1.call-done, bf16[2048,8192]{1,0:T(8,128)(2,1)} %all-gather.7.cloned.1.call-done, bf16[2,128,2048]{2,1,0:T(8,128)(2,1)S(1)} %copy-done.2, pred[]{:T(512)S(6)} %eq.2), kind=kOutput, calls=%fused_computation.470 | convolution fusion | flops 4295753728 | bytes 37748736 | tf_op jit(solution)/shard_map/dot_general | solution.py:135
  417.0 34.5 %all-reduce.6.cloned.1.call-done = f32[128,544]{0,1:T(8,128)} async-done(((f32[128,544]{0,1:T(8,128)}), f32[128,544]{0,1:T(8,128)}) %all-reduce.6.cloned.1.call-update) | async-done | bytes 278544 | tf_op jit(solution)/shard_map/psum | solution.py:76
  458.3 32.6 %while.112 = (s32[]{:T(128)}, f32[16,2048]{1,0:T(8,128)S(1)}, f32[16,8,2048]{2,1,0:T(8,128)}, f32[16,2048]{1,0:T(8,128)S(1)}, f32[16,8,16]{2,1,0:T(8,128)S(1)}, ...) while((s32[]{:T(128)}, f32[16,2048]{1,0:T(8,128)S(1)}, ...), condition=%wide.region_23.24_spmd.clone, body=%wide.region_22.23_spmd.clone.sunk | while | flops 1114122 | bytes 789263 | solution.py:58
  491.4 8.4 all-gather.1
  513.2 61.9 %while.108 = (s32[]{:T(128)}, f32[16,2048]{1,0:T(8,128)S(1)}, f32[16,8,2048]{2,1,0:T(8,128)}, f32[16,8,2048]{2,1,0:T(8,128)}, f32[16,2048]{1,0:T(8,128)S(1)}, /*...) while((s32[]{:T(128)}, f32[16,2048]{1,0:T(8,128)S(1)}, ...), condition=%wide.region_35.36_spmd, body=%wide.region_26.35_spmd.sunk | while | flops 2375689 | bytes 1874069 | solution.py:58
  578.0 17.1 %fusion.178 = f32[128,8192]{1,0:T(8,128)} fusion(bf16[128,2048]{1,0:T(8,128)(2,1)S(1)} %get-tuple-element.620, bf16[2048,8192]{1,0:T(8,128)(2,1)} %all-gather.7.cloned.1.call-done), kind=kOutput, calls=%fused_computation.475 | convolution fusion | flops 4294967296 | bytes 38273024 | tf_op jit(solution)/shard_map/dot_general | solution.py:153
  595.2 76.2 %reduce-scatter.5.cloned.1.call-done = f32[32,8192]{1,0:T(8,128)} async-done(((f32[128,8192]{1,0:T(8,128)}), f32[32,8192]{1,0:T(8,128)}) %reduce-scatter.5.cloned.1.call-update) | async-done | bytes 1048592 | tf_op jit(solution)/shard_map/reduce_scatter | solution.py:154
  676.0 10.6 %collective-permute-done.3 = bf16[32,8192]{1,0:T(8,128)(2,1)S(1)} collective-permute-done((bf16[32,8192]{1,0:T(8,128)(2,1)S(1)}, bf16[32,8192]{1,0:T(8,128)(2,1)S(1)}, u32[]{:S(2)}, u32[]{:S(2)}) %collective-permute-start.3) | collective-permute-done | bytes 524320 | tf_op jit(solution)/shard_map/ppermute | solution.py:10
  687.9 46.5 %all-gather.11.cloned.1.call-done = bf16[128,8192]{1,0:T(8,128)(2,1)} async-done(((bf16[32,8192]{1,0:T(8,128)(2,1)}), bf16[128,8192]{1,0:T(8,128)(2,1)}) %all-gather.11.cloned.1.call-update) | async-done | bytes 2097168 | tf_op jit(solution)/shard_map/all_gather | solution.py:134
  734.4 16.3 %fusion.175 = (f32[128,2048]{1,0:T(8,128)S(1)}, bf16[128,2048]{1,0:T(8,128)(2,1)S(1)}) fusion(bf16[128,8192]{1,0:T(8,128)(2,1)} %all-gather.11.cloned.1.call-done, bf16[2048,8192]{1,0:T(8,128)(2,1)} %all-gather.7.cloned.1.call-done, bf16[2,128,2048]{2,1,0:T(8,128)(2,1)S(1)} %copy-done.3, pred[]{:T(512)S(6)} %eq.2), kind=kOutput, calls=%fused_computation.472 | convolution fusion | flops 4295753728 | bytes 37748736 | tf_op jit(solution)/shard_map/dot_general | solution.py:135
  759.4 34.6 %all-reduce.8.cloned.1.call-done = f32[128,544]{0,1:T(8,128)} async-done(((f32[128,544]{0,1:T(8,128)}), f32[128,544]{0,1:T(8,128)}) %all-reduce.8.cloned.1.call-update) | async-done | bytes 278544 | tf_op jit(solution)/shard_map/psum | solution.py:76
  799.5 32.8 %while.113 = (s32[]{:T(128)}, f32[16,2048]{1,0:T(8,128)S(1)}, f32[16,8,2048]{2,1,0:T(8,128)}, f32[16,2048]{1,0:T(8,128)S(1)}, f32[16,8,16]{2,1,0:T(8,128)S(1)}, ...) while((s32[]{:T(128)}, f32[16,2048]{1,0:T(8,128)S(1)}, ...), condition=%wide.region_42.43_spmd.clone, body=%wide.region_41.42_spmd.clone.sunk | while | flops 1114122 | bytes 789263 | solution.py:58
  832.9 8.4 all-gather.2
  853.3 62.2 %while.110 = (s32[]{:T(128)}, f32[16,2048]{1,0:T(8,128)S(1)}, f32[16,8,2048]{2,1,0:T(8,128)}, f32[16,8,2048]{2,1,0:T(8,128)}, f32[16,2048]{1,0:T(8,128)S(1)}, /*...) while((s32[]{:T(128)}, f32[16,2048]{1,0:T(8,128)S(1)}, ...), condition=%wide.region_54.55_spmd, body=%wide.region_45.54_spmd.sunk | while | flops 2375689 | bytes 1874069 | solution.py:58
  (767 shorter events, 399.5 us)
Async XLA Ops:
  7.4 47.6 %all-reduce.4.cloned.1.call-start = ((), (), s32[]{:S(2)}) async-start(), calls=%async_computation.2 | async-start | bytes 557056 | tf_op jit(solution)/shard_map/psum | solution.py:76
  8.3 4.4 collective-permute-start
  18.4 216.0 %all-gather.7.cloned.1.call-start = ((), (), s32[]{:S(2)}) async-start(), calls=%async_computation.3 | async-start | bytes 41943040 | tf_op jit(solution)/shard_map/all_gather | solution.py:120
  25.7 303.3 %reduce-scatter.3.cloned.1.call-start = ((), (), s32[]{:S(2)}) async-start(), calls=%async_computation.4 | async-start | bytes 5242880 | tf_op jit(solution)/shard_map/reduce_scatter | solution.py:154
  123.3 63.8 %copy-start.17 = (f32[1,2048]{1,0:T(1,128)S(1)}, f32[1,2048]{1,0:T(1,128)}, u32[]{:S(2)}) copy-start(f32[1,2048]{1,0:T(1,128)} %param.43) | copy-start | bytes 24580
  251.5 92.9 %copy-start.13 = (f32[8192]{0:T(1024)S(1)}, f32[8192]{0:T(1024)}, u32[]{:S(2)}) copy-start(f32[8192]{0:T(1024)} %param.36) | copy-start | bytes 98308
  251.5 140.5 %copy-start.2 = (bf16[2,128,2048]{2,1,0:T(8,128)(2,1)S(1)}, bf16[2,128,2048]{2,1,0:T(8,128)(2,1)}, u32[]{:S(2)}) copy-start(bf16[2,128,2048]{2,1,0:T(8,128)(2,1)} %param.31) | copy-start | bytes 3145732
  251.6 140.5 %all-gather.9.cloned.1.call-start = ((), (), s32[]{:S(2)}) async-start(), calls=%async_computation.5 | async-start | bytes 2621440 | tf_op jit(solution)/shard_map/all_gather | solution.py:134
  330.4 13.7 %collective-permute-start.1 = (bf16[32,8192]{1,0:T(8,128)(2,1)S(1)}, bf16[32,8192]{1,0:T(8,128)(2,1)S(1)}, u32[]{:S(2)}, u32[]{:S(2)}) collective-permute-start(bf16[32,8192]{1,0:T(8,128)(2,1)S(1)} %fusion.156), channel_id=1, source_target_pairs={{0,16},{1,17},{2,18},{3,19},{4,20},{5,21},{6,22},{7,23},{8,24},{9,... | collective-permute-start | bytes 1572872 | tf_op jit(solution)/shard_map/ppermute | solution.py:10
  345.4 66.4 %copy-start.8 = (f32[1,1,2048]{2,1,0:T(1,128)S(1)}, f32[1,1,2048]{2,1,0:T(1,128)}, u32[]{:S(2)}) copy-start(f32[1,1,2048]{2,1,0:T(1,128)} %copy-done.7) | copy-start | bytes 24580
  345.4 66.4 %copy-start.11 = (f32[1,1,2048]{2,1,0:T(1,128)S(1)}, f32[1,1,2048]{2,1,0:T(1,128)}, u32[]{:S(2)}) copy-start(f32[1,1,2048]{2,1,0:T(1,128)} %copy-done.10) | copy-start | bytes 24580
  345.5 66.4 %copy-start.15 = (f32[1,2048]{1,0:T(1,128)S(1)}, f32[1,2048]{1,0:T(1,128)}, u32[]{:S(2)}) copy-start(f32[1,2048]{1,0:T(1,128)} %param.38) | copy-start | bytes 24580
  345.5 106.1 %all-reduce.6.cloned.1.call-start = ((), (), s32[]{:S(2)}) async-start(), calls=%async_computation.6 | async-start | bytes 557056 | tf_op jit(solution)/shard_map/psum | solution.py:76
  408.3 3.5 collective-permute-start.2
  415.1 256.3 %reduce-scatter.5.cloned.1.call-start = ((), (), s32[]{:S(2)}) async-start(), calls=%async_computation.7 | async-start | bytes 5242880 | tf_op jit(solution)/shard_map/reduce_scatter | solution.py:154
  595.2 91.7 %copy-start.14 = (f32[8192]{0:T(1024)S(1)}, f32[8192]{0:T(1024)}, u32[]{:S(2)}) copy-start(f32[8192]{0:T(1024)} %param.36) | copy-start | bytes 98308
  595.2 139.3 %copy-start.3 = (bf16[2,128,2048]{2,1,0:T(8,128)(2,1)S(1)}, bf16[2,128,2048]{2,1,0:T(8,128)(2,1)}, u32[]{:S(2)}) copy-start(bf16[2,128,2048]{2,1,0:T(8,128)(2,1)} %param.31) | copy-start | bytes 3145732
  595.2 139.2 %all-gather.11.cloned.1.call-start = ((), (), s32[]{:S(2)}) async-start(), calls=%async_computation.8 | async-start | bytes 2621440 | tf_op jit(solution)/shard_map/all_gather | solution.py:134
  672.9 13.7 %collective-permute-start.3 = (bf16[32,8192]{1,0:T(8,128)(2,1)S(1)}, bf16[32,8192]{1,0:T(8,128)(2,1)S(1)}, u32[]{:S(2)}, u32[]{:S(2)}) collective-permute-start(bf16[32,8192]{1,0:T(8,128)(2,1)S(1)} %fusion.155), channel_id=1, source_target_pairs={{0,16},{1,17},{2,18},{3,19},{4,20},{5,21},{6,22},{7,23},{8,24},{9,... | collective-permute-start | bytes 1572872 | tf_op jit(solution)/shard_map/ppermute | solution.py:10
  687.9 66.4 %copy-start.9 = (f32[1,1,2048]{2,1,0:T(1,128)S(1)}, f32[1,1,2048]{2,1,0:T(1,128)}, u32[]{:S(2)}) copy-start(f32[1,1,2048]{2,1,0:T(1,128)} %copy-done.7) | copy-start | bytes 24580
  687.9 66.4 %copy-start.12 = (f32[1,1,2048]{2,1,0:T(1,128)S(1)}, f32[1,1,2048]{2,1,0:T(1,128)}, u32[]{:S(2)}) copy-start(f32[1,1,2048]{2,1,0:T(1,128)} %copy-done.10) | copy-start | bytes 24580
  687.9 66.4 %copy-start.16 = (f32[1,2048]{1,0:T(1,128)S(1)}, f32[1,2048]{1,0:T(1,128)}, u32[]{:S(2)}) copy-start(f32[1,2048]{1,0:T(1,128)} %param.38) | copy-start | bytes 24580
  687.9 106.0 %all-reduce.8.cloned.1.call-start = ((), (), s32[]{:S(2)}) async-start(), calls=%async_computation.9 | async-start | bytes 557056 | tf_op jit(solution)/shard_map/psum | solution.py:76
  750.7 3.5 collective-permute-start.4
  (12 other events, 265.4 us)
Sparse Core Ops, SparseCore 0:
  18.5 36.4 all-reduce.3
  251.7 77.2 reduce-scatter.2
  345.6 46.4 all-gather.8
  415.2 36.3 all-reduce.5
  595.3 76.0 reduce-scatter.4
  688.0 46.3 all-gather.10
  757.6 36.2 all-reduce.7
Sparse Core Ops, SparseCore 1:
  25.8 208.6 all-gather.6
where the time goes:
time: 937 us; the launch traced here: 926 us
  waiting for transfers between devices  415 us (44%)
  other arithmetic  257 us (27%)
  local copies, waits for them, and re-layouts  86.5 us (9%)
  matrix products  83.5 us (9%)
  blocking collectives  54.9 us (6%)
  between operations  15.4 us (2%)
  starting transfers between devices  10.8 us (1%)
    mul x96, other arithmetic, fold_block(): step_rows[inner] * act_rows[inner]  166 us
    reduce_scatter x2, waiting for transfers between devices, shards(): lax.psum_scatter(partial_link, 'tp', scatter_dimension=0, tiled=True)  154 us
    psum x3, waiting for transfers between devices, run_section(): projected = lax.psum(partial_proj, 'tp')  98.3 us
    all_gather x2, waiting for transfers between devices, shards(): normed = lax.all_gather(normed_share, 'tp', axis=0, tiled=True)  92.8 us
    all_gather x6, blocking collectives, entering(): gathered = jax.tree.map(lambda a: lax.all_gather(a, axis), part)  54.9 us
    all_gather x1, waiting for transfers between devices, shards(): link_full = lax.all_gather(own_link, 'ctx', axis=1, tiled=True)  44.6 us
    dot_general x2, matrix products, shards(): partial_link = jnp.dot(mixed, link_full, preferred_element_type=jnp.float32)  34.2 us
    reduce_sum x144, other arithmetic, fold_block(): outputs.append(jnp.sum(out_rows[inner][:, None] * state, axis=0))  34.1 us
  transfers between devices with their start and end apart: 13, of which 12 were waited for; matrix products, arithmetic and copies ran while one was open for 13% of the time, Pallas kernels for 0%

commit v1 on v0

v1 whole, which is shorter than its diff:
```python
import functools

import jax
import jax.numpy as jnp
from jax import lax
from jax.experimental import pallas as pl
from jax.experimental.pallas import tpu as pltpu
from jax.sharding import PartitionSpec as P

LANES = 128
TILE = 1024
ROWS = 8
LOG2E = 1.4426950408889634
BF16 = jnp.bfloat16
F32 = jnp.float32


def params():
    return pltpu.CompilerParams(vmem_limit_bytes=32 * 1024 * 1024)


def rotated(block, axis, distance):
    count = lax.axis_size(axis)
    return lax.ppermute(block, axis, [(i, (i + distance) % count) for i in range(count)])


def shifted(block, axis, distance):
    count = lax.axis_size(axis)
    return lax.ppermute(block, axis, [(i - distance, i) for i in range(distance, count)])


def swapped(block):
    return lax.ppermute(block, "pipe", [(0, 1), (1, 0)])


def sibling(block):
    count = lax.axis_size("ctx")
    return lax.ppermute(block, "ctx", [(i, i ^ 1) for i in range(count)])


def swap_shared(weight):
    half = weight.shape[0] // 2
    core = lax.axis_index("ctx") % 2
    part = swapped(lax.dynamic_slice_in_dim(weight, core * half, half, 0))
    rest = sibling(part)
    first = core == 0
    return jnp.concatenate([jnp.where(first, part, rest), jnp.where(first, rest, part)], axis=0)


def conv_kernel(x_ref, rim_ref, w_ref, b_ref, proj_ref, act_ref, part_ref, pad, total):
    count, width = x_ref.shape
    taps = w_ref.shape[0]
    rim = rim_ref.shape[0]
    pad[:rim, :] = rim_ref[...].astype(F32)
    pad[rim:, :] = x_ref[...].astype(F32)
    for row in range(0, count, 32):
        value = b_ref[...] + jnp.zeros((32, width), F32)
        for k in range(taps):
            start = rim - (taps - 1) + row + k
            value = value + w_ref[k : k + 1, :] * pad[start : start + 32, :]
        act_ref[row : row + 32, :] = (value / (1.0 + jnp.exp(-value))).astype(BF16)
    product = jnp.dot(act_ref[...], proj_ref[...], preferred_element_type=F32)
    step = pl.program_id(0)

    @pl.when(step == 0)
    def _():
        total[...] = product

    @pl.when(step > 0)
    def _():
        total[...] += product

    @pl.when(step == pl.num_programs(0) - 1)
    def _():
        part_ref[...] = total[...].astype(BF16)


def conv_project(inputs, rim, conv_weight, conv_bias, x_proj):
    count, width = inputs.shape
    cols = x_proj.shape[1]
    block = 512
    return pl.pallas_call(
        conv_kernel,
        grid=(width // block,),
        in_specs=[
            pl.BlockSpec((count, block), lambda c: (0, c)),
            pl.BlockSpec((rim.shape[0], block), lambda c: (0, c)),
            pl.BlockSpec((conv_weight.shape[0], block), lambda c: (0, c)),
            pl.BlockSpec((1, block), lambda c: (0, c)),
            pl.BlockSpec((block, cols), lambda c: (c, 0)),
        ],
        out_specs=[
            pl.BlockSpec((count, block), lambda c: (0, c)),
            pl.BlockSpec((count, cols), lambda c: (0, 0)),
        ],
        out_shape=[
            jax.ShapeDtypeStruct((count, width), BF16),
            jax.ShapeDtypeStruct((count, cols), BF16),
        ],
        scratch_shapes=[
            pltpu.VMEM((count + rim.shape[0], block), F32),
            pltpu.VMEM((count, cols), F32),
        ],
        compiler_params=params(),
        name="conv_project",
    )(inputs, rim, conv_weight, conv_bias, x_proj)


def scan_kernel(nstate, maps_ref, rate_ref, dt_ref, bias_ref, act_ref, decay_ref,
                resp_ref, cum_ref, end_ref, steps, driven, wide):
    count = rate_ref.shape[0]
    wide[...] = jnp.dot(rate_ref[...], dt_ref[...], preferred_element_type=F32)

    def spread(group, carry):
        base = pl.multiple_of(group * 16, 16)
        for j in range(ROWS):
            lanes = slice(j * LANES, (j + 1) * LANES)
            raw = wide[pl.ds(base, 16), lanes] + bias_ref[:, lanes]
            rate = jnp.maximum(raw, 0.0) + jnp.log1p(jnp.exp(-jnp.abs(raw)))
            active = act_ref[pl.ds(base, 16), lanes].astype(F32)
            steps[pl.ds(base * ROWS + j, 16, stride=ROWS), :] = rate
            driven[pl.ds(base * ROWS + j, 16, stride=ROWS), :] = rate * active
        return carry

    lax.fori_loop(0, count // 16, spread, 0)

    def one(t, carry):
        state, cum = carry
        rows = pl.ds(pl.multiple_of(t * ROWS, ROWS), ROWS)
        rate = steps[rows, :]
        drive = driven[rows, :]
        later, sums = [], [None] * 4
        for n in range(nstate):
            h = jnp.exp2(rate * decay_ref[n]) * state[n] + maps_ref[t, n] * drive
            later.append(h)
            term = maps_ref[t, nstate + n] * h
            sums[n % 4] = term if sums[n % 4] is None else sums[n % 4] + term
        cum = cum + rate
        resp_ref[rows, :] = (sums[0] + sums[1]) + (sums[2] + sums[3])
        cum_ref[rows, :] = cum
        return tuple(later), cum

    def pair(g, carry):
        return one(2 * g + 1, one(2 * g, carry))

    zero = jnp.zeros((ROWS, LANES), F32)
    state, cum = lax.fori_loop(0, count // 2, pair, ((zero,) * nstate, zero))
    for n in range(nstate):
        end_ref[n] = state[n]
    end_ref[nstate] = cum


def local_scan(maps, rate_normed, dt_proj, dt_bias, activated, decay):
    count, width = activated.shape
    rank = dt_proj.shape[0]
    nstate = decay.shape[0]
    tiles = width // TILE
    rows = pl.BlockSpec((None, count * ROWS, LANES), lambda c: (c, 0, 0))
    return pl.pallas_call(
        functools.partial(scan_kernel, nstate),
        grid=(tiles,),
        in_specs=[
            pl.BlockSpec(memory_space=pltpu.SMEM),
            pl.BlockSpec((count, rank), lambda c: (0, 0)),
            pl.BlockSpec((rank, TILE), lambda c: (0, c)),
            pl.BlockSpec((1, TILE), lambda c: (0, c)),
            pl.BlockSpec((count, TILE), lambda c: (0, c)),
            pl.BlockSpec((nstate, ROWS, LANES), lambda c: (0, c, 0)),
        ],
        out_specs=[rows, rows, pl.BlockSpec((nstate + 1, ROWS, LANES), lambda c: (0, c, 0))],
        out_shape=[
            jax.ShapeDtypeStruct((tiles, count * ROWS, LANES), F32),
            jax.ShapeDtypeStruct((tiles, count * ROWS, LANES), F32),
            jax.ShapeDtypeStruct((nstate + 1, tiles * ROWS, LANES), F32),
        ],
        scratch_shapes=[
            pltpu.VMEM((count * ROWS, LANES), F32),
            pltpu.VMEM((count * ROWS, LANES), F32),
            pltpu.VMEM((count, TILE), F32),
        ],
        compiler_params=params(),
        name="local_scan",
    )(maps, rate_normed, dt_proj, dt_bias, activated, decay)


def finish_kernel(nstate, earlier, maps_ref, resp_ref, cum_ref, decay_ref, skip_ref,
                  act_ref, gate_ref, *rest):
    ends, out_ref, total, enter = rest[:earlier], rest[earlier], rest[earlier + 1], rest[earlier + 2]
    count = act_ref.shape[0]
    for n in range(nstate):
        value, passed = ends[0][n], ends[0][nstate]
        for block in ends[1:]:
            value = value + jnp.exp2(decay_ref[n] * passed) * block[n]
            passed = passed + block[nstate]
        enter[n] = value

    def one(t):
        rows = pl.ds(pl.multiple_of(t * ROWS, ROWS), ROWS)
        cum = cum_ref[rows, :]
        sums = [resp_ref[rows, :], None, None, None]
        for n in range(nstate):
            term = maps_ref[t, nstate + n] * (jnp.exp2(cum * decay_ref[n]) * enter[n])
            sums[n % 4] = term if sums[n % 4] is None else sums[n % 4] + term
        total[rows, :] = (sums[0] + sums[1]) + (sums[2] + sums[3])

    def pair(g, carry):
        one(2 * g)
        one(2 * g + 1)
        return carry

    lax.fori_loop(0, count // 2, pair, 0)

    def gather(group, carry):
        base = pl.multiple_of(group * 16, 16)
        for j in range(ROWS):
            lanes = slice(j * LANES, (j + 1) * LANES)
            active = act_ref[pl.ds(base, 16), lanes].astype(F32)
            gate = gate_ref[pl.ds(base, 16), lanes].astype(F32)
            value = total[pl.ds(base * ROWS + j, 16, stride=ROWS), :] + skip_ref[:, lanes] * active
            out_ref[pl.ds(base, 16), lanes] = (value * (gate / (1.0 + jnp.exp(-gate)))).astype(BF16)
        return carry

    lax.fori_loop(0, count // 16, gather, 0)


def finish(maps, response, cum, decay, skip, activated, gate, ends):
    count, width = activated.shape
    nstate = decay.shape[0]
    rows = pl.BlockSpec((None, count * ROWS, LANES), lambda c: (c, 0, 0))
    flat = pl.BlockSpec((count, TILE), lambda c: (0, c))
    return pl.pallas_call(
        functools.partial(finish_kernel, nstate, len(ends)),
        grid=(width // TILE,),
        in_specs=[
            pl.BlockSpec(memory_space=pltpu.SMEM),
            rows,
            rows,
            pl.BlockSpec((nstate, ROWS, LANES), lambda c: (0, c, 0)),
            pl.BlockSpec((1, TILE), lambda c: (0, c)),
            flat,
            flat,
        ]
        + [pl.BlockSpec((nstate + 1, ROWS, LANES), lambda c: (0, c, 0))] * len(ends),
        out_specs=flat,
        out_shape=jax.ShapeDtypeStruct((count, width), BF16),
        scratch_shapes=[
            pltpu.VMEM((count * ROWS, LANES), F32),
            pltpu.VMEM((nstate, ROWS, LANES), F32),
        ],
        compiler_params=params(),
        name="finish_mixer",
    )(maps, response, cum, decay, skip, activated, gate, *ends)


def mixer(inputs, gate, small, x_proj, dt_proj):
    conv_weight, conv_bias, dt_bias, decay, skip = small
    rank = dt_proj.shape[0]
    nstate = decay.shape[0]
    rim = shifted(inputs[-16:], "ctx", 1)
    activated, partial = conv_project(inputs, rim, conv_weight, conv_bias, x_proj)
    parts = [partial] + [rotated(partial, "tp", s) for s in range(1, lax.axis_size("tp"))]
    projected = parts[0].astype(F32)
    for part in parts[1:]:
        projected = projected + part.astype(F32)
    low = projected[:, :rank]
    rate_normed = (
        low * lax.rsqrt(jnp.mean(low * low, axis=1, keepdims=True) + 1e-06)
    ).astype(BF16)
    maps = projected[:, rank:]
    decay_tiles = (decay * -LOG2E).reshape(nstate, -1, LANES)
    response, cum, end = local_scan(maps, rate_normed, dt_proj, dt_bias, activated, decay_tiles)
    ends = [shifted(end, "ctx", s) for s in range(1, lax.axis_size("ctx"))]
    return finish(maps, response, cum, decay_tiles, skip, activated, gate, ends)


def shards(
    x_in,
    hidden_in,
    gate_z,
    out_proj,
    in_proj,
    norm_gain,
    conv_weight,
    conv_bias,
    x_proj,
    dt_proj,
    dt_bias,
    decay_rate,
    skip,
):
    segment = lax.axis_index("pipe")
    first = segment == 0
    ctx, tp = lax.axis_size("ctx"), lax.axis_size("tp")
    place, column = lax.axis_index("ctx"), lax.axis_index("tp")
    block = hidden_in.shape[1]
    depth = out_proj.shape[1]
    width = x_in.shape[2]

    own_small = jnp.concatenate(
        [conv_weight[0], conv_bias, dt_bias, decay_rate[0], skip], axis=0
    )
    other_small = swapped(own_small)
    other_x = swap_shared(x_proj[0])
    held_dt, other_x = lax.optimization_barrier((dt_proj[0], other_x))
    other_dt = swap_shared(held_dt)
    own_gate = lax.dynamic_index_in_dim(gate_z[0], segment, 0, False)
    held_gate, other_dt = lax.optimization_barrier(
        (lax.dynamic_index_in_dim(gate_z[0], 1 - segment, 0, False), other_dt)
    )
    other_gate = swapped(held_gate)
    taps = conv_weight.shape[1]
    nstate = decay_rate.shape[1]

    def weights(section):
        mine = first if section == 0 else jnp.logical_not(first)
        small = jnp.where(mine, own_small, other_small)
        parts = (
            small[:taps],
            small[taps : taps + 1],
            small[taps + 1 : taps + 2],
            small[taps + 2 : taps + 2 + nstate],
            small[taps + 2 + nstate :],
        )
        return (
            jnp.where(mine, own_gate, other_gate),
            parts,
            jnp.where(mine, x_proj[0], other_x),
            jnp.where(mine, dt_proj[0], other_dt),
        )

    inputs = lax.dynamic_index_in_dim(x_in, segment, 0, False)
    mixed_first = mixer(inputs, *weights(0))
    kept_first = lax.ppermute(mixed_first, "pipe", [(1, 0)])

    hidden = lax.dynamic_index_in_dim(hidden_in, segment, 0, False)
    hidden_parts = []
    for s in range(ctx):
        target = lax.rem(place + s, ctx)
        piece = lax.dynamic_slice_in_dim(hidden, target * depth, depth, 1)
        hidden_parts.append(piece if s == 0 else rotated(piece, "ctx", s))
    hidden_rows = jnp.stack(hidden_parts, axis=0)

    every = jnp.stack(
        [mixed_first] + [rotated(mixed_first, "ctx", s) for s in range(1, ctx)], axis=0
    ).reshape(ctx, tp, block, width)
    link = None
    for s in reversed(range(tp)):
        target = lax.rem(column + s, tp)
        rows = lax.dynamic_index_in_dim(every, target, 1, False).reshape(ctx * block, width)
        product = jnp.dot(rows, out_proj, preferred_element_type=F32)
        part = product if s == 0 else rotated(product.astype(BF16), "tp", s)
        link = part.astype(F32) if link is None else link + part.astype(F32)
    carried = (hidden_rows.reshape(ctx * block, depth).astype(F32) + link).astype(BF16)
    wide = carried.astype(F32)
    order = lax.rem(place - jnp.arange(ctx) + ctx, ctx)
    square = jnp.sum(wide * wide, axis=1).reshape(ctx, block)[order]
    squares = square
    for s in range(1, ctx):
        squares = squares + rotated(square, "ctx", s)
    scale = lax.rsqrt(squares[order].reshape(-1, 1) / (depth * ctx) + 1e-05)
    gain = lax.dynamic_slice_in_dim(norm_gain, place * depth, depth, 0)
    normed = (wide * scale * gain[None, :]).astype(BF16)

    products = []
    for s in range(tp):
        part = normed if s == 0 else rotated(normed, "tp", s)
        products.append(
            lax.dot_general(
                part, in_proj, (((1,), (1,)), ((), ())), preferred_element_type=F32
            ).reshape(ctx, block, width)
        )
    made = None
    for s in range(ctx):
        rows = jnp.stack([product[s] for product in products], axis=0)
        part = rows if s == 0 else rotated(rows.astype(BF16), "ctx", -s)
        made = part.astype(F32) if made is None else made + part.astype(F32)
    made = made.astype(BF16)
    inputs = jnp.concatenate(
        [
            lax.dynamic_index_in_dim(made, lax.rem(column - k + tp, tp), 0, False)
            for k in range(tp)
        ],
        axis=0,
    )
    mixed_second = mixer(inputs, *weights(1))
    kept_second = lax.ppermute(mixed_second, "pipe", [(0, 1)])
    low = jnp.where(first, mixed_first, kept_second)
    high = jnp.where(first, kept_first, mixed_second)
    return jnp.stack([low, high], axis=0)[None]


def solution(mesh):
    in_specs = (
        P(None, "ctx", "tp"),
        P(None, ("ctx", "tp"), None),
        P("pipe", None, "ctx", "tp"),
        P("tp", "ctx"),
        P("tp", "ctx"),
        P(),
        P("pipe", None, "tp"),
        P("pipe", "tp"),
        P("pipe", "tp", None),
        P("pipe", None, "tp"),
        P("pipe", "tp"),
        P("pipe", None, "tp"),
        P("pipe", "tp"),
    )
    out_specs = P("pipe", None, "ctx", "tp")
    return jax.shard_map(shards, mesh=mesh, in_specs=in_specs, out_specs=out_specs, check_vma=False)
```

time: 937 us -> 343 us (0.37)
  other arithmetic: 257 us -> 11.8 us
  waiting for transfers between devices: 415 us -> 182 us
  local copies, waits for them, and re-layouts: 86.5 us -> 20.2 us
  blocking collectives: 54.9 us -> 0 us
  matrix products: 83.5 us -> 34.9 us
  starting transfers between devices: 10.8 us -> 53 us
  Pallas kernels: 0 us -> 37.4 us
  between operations: 15.4 us -> 0.71 us
    mul x96 -> x0, other arithmetic: 166 us -> none  [fold_block(): step_rows[inner] * act_rows[inner]]
    ppermute x5 -> x40, waiting for transfers between devices: 25.4 us -> 182 us  [the longest x24 115 us: rotated(): lax.ppermute(block, axis, [(i, (i + distance) % count) for i in range(cou...]
    reduce_scatter x2 -> x0, waiting for transfers between devices: 154 us -> none  [shards(): lax.psum_scatter(partial_link, 'tp', scatter_dimension=0, tiled=True)]
    all_gather x3 -> x0, waiting for transfers between devices: 137 us -> none  [the longest x2 92.8 us: shards(): normed = lax.all_gather(normed_share, 'tp', axis=0, tiled=True)]
    psum x3 -> x0, waiting for transfers between devices: 98.3 us -> none  [run_section(): projected = lax.psum(partial_proj, 'tp')]
    all_gather x6 -> x0, blocking collectives: 54.9 us -> none  [entering(): gathered = jax.tree.map(lambda a: lax.all_gather(a, axis), part)]
    dot_general x10 -> x8, matrix products: 83.5 us -> 34.9 us  [the longest x4 18.5 us: shards(): lax.dot_general(part, in_proj, (((1,), (1,)), ((), ())), preferred_elemen...]
    ppermute x5 -> x40, starting transfers between devices: 10.4 us -> 53 us  [the longest x24 32 us: rotated(): lax.ppermute(block, axis, [(i, (i + distance) % count) for i in range(cou...]
  transfers between devices with their start and end apart: 13 -> 40, of which waited for: 12 -> 24; matrix products, arithmetic and copies ran while one was open for 13% -> 14% of each run, Pallas kernels for 0% -> 8%
where the time goes in v1:
time: 343 us; the launch traced here: 340 us
  waiting for transfers between devices  182 us (53%)
  starting transfers between devices  53 us (15%)
  Pallas kernels  37.4 us (11%)
  matrix products  34.9 us (10%)
  local copies, waits for them, and re-layouts  20.2 us (6%)
  other arithmetic  11.8 us (3%)
    ppermute x24, waiting for transfers between devices, rotated(): lax.ppermute(block, axis, [(i, (i + distance) % count) for i in range(cou...  115 us
    ppermute x4, waiting for transfers between devices, swapped(): return lax.ppermute(block, 'pipe', [(0, 1), (1, 0)])  39.3 us
    ppermute x24, starting transfers between devices, rotated(): lax.ppermute(block, axis, [(i, (i + distance) % count) for i in range(cou...  32 us
    pallas_call x2, Pallas kernels, local_scan(): pl.pallas_call(functools.partial(scan_kernel, nstate), grid=(tiles,), in_...  19.1 us
    dot_general x4, matrix products, shards(): lax.dot_general(part, in_proj, (((1,), (1,)), ((), ())), preferred_elemen...  18.5 us
    dot_general x4, matrix products, shards(): product = jnp.dot(rows, out_proj, preferred_element_type=F32)  16.4 us
    ppermute x8, waiting for transfers between devices, shifted(): lax.ppermute(block, axis, [(i - distance, i) for i in range(distance, cou...  15.6 us
    pallas_call x2, Pallas kernels, finish(): pl.pallas_call(functools.partial(finish_kernel, nstate, len(ends)), grid=...  13.7 us
  transfers between devices with their start and end apart: 40, of which 24 were waited for; matrix products, arithmetic and copies ran while one was open for 14% of the time, Pallas kernels for 8%

profile of v1, /device:TPU:11, one launch (start us, length us, event | category | flops | bytes accessed | tf_op | source)
XLA Modules:
  0.0 340.2 jit_solution(4233123868742163951)
XLA Ops:
  2.7 24.3 %collective-permute-done.2 = bf16[1024,544]{0,1:T(8,128)(2,1)} collective-permute-done((bf16[1024,544]{0,1:T(8,128)(2,1)S(1)}, bf16[1024,544]{0,1:T(8,128)(2,1)}, u32[]{:S(2)}, u32[]{:S(2)}) %collective-permute-start.2) | collective-permute-done | bytes 1114144 | tf_op jit(solution)/shard_map/ppermute | solution.py:33
  33.8 4.4 %copy.16 = bf16[1,2048,544]{2,1,0:T(8,128)(2,1)} copy(bf16[1,2048,544]{1,2,0:T(8,128)(2,1)} %param.21) | data formatting | bytes 4456448 | tf_op args[8]
  53.8 15.0 %collective-permute-done.7 = bf16[256,2048]{1,0:T(8,128)(2,1)S(1)} collective-permute-done((bf16[256,2048]{1,0:T(8,128)(2,1)S(1)}, bf16[256,2048]{1,0:T(8,128)(2,1)S(1)}, u32[]{:S(2)}, u32[]{:S(2)}) %collective-permute-start.7) | collective-permute-done | bytes 1048608 | tf_op jit(solution)/shard_map/ppermute | solution.py:33
  76.4 9.5 %local_scan.2 = (f32[2,1024,128]{2,1,0:T(8,128)S(1)}, f32[2,1024,128]{2,1,0:T(8,128)S(1)}, f32[17,16,128]{2,1,0:T(8,128)S(1)}) custom-call(f32[128,32]{1,0:T(8,128)S(1)} %slice.218.maps_ref, bf16[128,512]{1,0:T(8,128)(2,1)S(1)} %multiply_convert_fusion.1.rate_ref, bf16[512,2048]{1,0:T(8,128)(2,1)S(1)} %get-tuple-element.38.dt_ref, ...), custom_call_target="tpu_custom_call" | custom-call | tf_op jit(solution)/shard_map/local_scan/pallas_call | solution.py:159
  90.7 5.5 %collective-permute-done.11.rest_1_ = f32[17,16,128]{2,1,0:T(8,128)S(1)} collective-permute-done((f32[17,16,128]{2,1,0:T(8,128)S(1)}, f32[17,16,128]{2,1,0:T(8,128)S(1)}, u32[]{:S(2)}, u32[]{:S(2)}) %collective-permute-start.11) | collective-permute-done | bytes 139296 | tf_op jit(solution)/shard_map/ppermute | solution.py:29
  97.9 6.9 %finish_mixer.2 = bf16[128,2048]{1,0:T(8,128)(2,1)S(1)} custom-call(f32[128,32]{1,0:T(8,128)S(1)} %slice.218.maps_ref, f32[2,1024,128]{2,1,0:T(8,128)S(1)} %get-tuple-element.24.resp_ref, f32[2,1024,128]{2,1,0:T(8,128)S(1)} %get-tuple-element.25.cum_ref, f32[16,16,128]{2,1,0:T(8,128)S(1)} %bitcast.114, f32[1,2048]{1,0:T(1,128)S(1)} %get-tuple-element.74.skip_ref, ...), custom_call_target="tpu_custom_call" | custom-call | tf_op jit(solution)/shard_map/finish_mixer/pallas_call | solution.py:231
  109.1 10.3 %collective-permute-done.18 = bf16[128,2048]{1,0:T(8,128)(2,1)} collective-permute-done((bf16[128,2048]{1,0:T(8,128)(2,1)S(1)}, bf16[128,2048]{1,0:T(8,128)(2,1)}, u32[]{:S(2)}, u32[]{:S(2)}) %collective-permute-start.18) | collective-permute-done | bytes 524320 | tf_op jit(solution)/shard_map/ppermute | solution.py:24
  119.4 8.5 %collective-permute-done.16 = bf16[128,2048]{1,0:T(8,128)(2,1)} collective-permute-done((bf16[128,2048]{1,0:T(8,128)(2,1)S(1)}, bf16[128,2048]{1,0:T(8,128)(2,1)}, u32[]{:S(2)}, u32[]{:S(2)}) %collective-permute-start.16) | collective-permute-done | bytes 524320 | tf_op jit(solution)/shard_map/ppermute | solution.py:24
  130.5 5.9 %convolution_convert_fusion = bf16[128,2048]{1,0:T(8,128)(2,1)} fusion(bf16[128,2048]{1,0:T(8,128)(2,1)S(1)} %bitcast.124, bf16[2048,2048]{1,0:T(8,128)(2,1)} %param.16), kind=kOutput, calls=%fused_computation.5 | convolution fusion | flops 1074003968 | bytes 9437184 | tf_op jit(solution)/shard_map/dot_general | solution.py:350
  153.3 27.0 %collective-permute-done.20 = bf16[128,2048]{1,0:T(8,128)(2,1)} collective-permute-done((bf16[128,2048]{1,0:T(8,128)(2,1)}, bf16[128,2048]{1,0:T(8,128)(2,1)}, u32[]{:S(2)}, u32[]{:S(2)}) %collective-permute-start.20) | collective-permute-done | bytes 524320 | tf_op jit(solution)/shard_map/ppermute | solution.py:24
  180.2 5.0 %collective-permute-done.19 = bf16[128,2048]{1,0:T(8,128)(2,1)} collective-permute-done((bf16[128,2048]{1,0:T(8,128)(2,1)}, bf16[128,2048]{1,0:T(8,128)(2,1)}, u32[]{:S(2)}, u32[]{:S(2)}) %collective-permute-start.19) | collective-permute-done | bytes 524320 | tf_op jit(solution)/shard_map/ppermute | solution.py:24
  185.2 6.3 %fusion = (f32[128]{0:T(128)S(1)}, bf16[128,2048]{1,0:T(8,128)(2,1)}) fusion(bf16[128,2048]{1,0:T(8,128)(2,1)} %collective-permute-done.21, bf16[128,2048]{1,0:T(8,128)(2,1)} %collective-permute-done.20, bf16[128,2048]{1,0:T(8,128)(2,1)} %collective-permute-done.19, bf16[4,32,2048]{2,1,0:T(8,128)(2,1)S(1)} %pad_maximum_fusion.3, ...), kind=kOutput, calls=%fused_computation.17 | convolution fusion | flops 1076887424 | bytes 11534848 | tf_op jit(solution)/shard_map/dot_general | solution.py:350
  200.8 6.4 %fusion.17 = (bf16[128,2048]{1,0:T(8,128)(2,1)S(1)}, f32[128,2048]{1,0:T(8,128)S(1)}) fusion(bf16[128,2048]{1,0:T(8,128)(2,1)S(1)} %fusion.2, bf16[2048,2048]{1,0:T(8,128)(2,1)} %param.17), kind=kOutput, calls=%fused_computation.98 | convolution fusion | flops 1074003968 | bytes 10485760 | tf_op jit(solution)/shard_map/dot_general | solution.py:368
  211.5 6.3 %fusion.14 = (bf16[128,2048]{1,0:T(8,128)(2,1)S(1)}, f32[128,2048]{1,0:T(8,128)S(1)}) fusion(bf16[128,2048]{1,0:T(8,128)(2,1)S(1)} %collective-permute-done.27, bf16[2048,2048]{1,0:T(8,128)(2,1)} %param.17), kind=kOutput, calls=%fused_computation.95 | convolution fusion | flops 1074003968 | bytes 10485760 | tf_op jit(solution)/shard_map/dot_general | solution.py:368
  217.8 14.0 %collective-permute-done.26 = bf16[128,2048]{1,0:T(8,128)(2,1)S(1)} collective-permute-done((bf16[128,2048]{1,0:T(8,128)(2,1)S(1)}, bf16[128,2048]{1,0:T(8,128)(2,1)S(1)}, u32[]{:S(2)}, u32[]{:S(2)}) %collective-permute-start.26) | collective-permute-done | bytes 524320 | tf_op jit(solution)/shard_map/ppermute | solution.py:24
  234.7 8.3 %collective-permute-done.25 = bf16[128,2048]{1,0:T(8,128)(2,1)S(1)} collective-permute-done((bf16[128,2048]{1,0:T(8,128)(2,1)S(1)}, bf16[128,2048]{1,0:T(8,128)(2,1)S(1)}, u32[]{:S(2)}, u32[]{:S(2)}) %collective-permute-start.25) | collective-permute-done | bytes 524320 | tf_op jit(solution)/shard_map/ppermute | solution.py:24
  250.7 10.3 %collective-permute-done.30 = bf16[4,32,2048]{2,1,0:T(8,128)(2,1)S(1)} collective-permute-done((bf16[4,32,2048]{2,1,0:T(8,128)(2,1)S(1)}, bf16[4,32,2048]{2,1,0:T(8,128)(2,1)S(1)}, u32[]{:S(2)}, u32[]{:S(2)}) %collective-permute-start.30) | collective-permute-done | bytes 524320 | tf_op jit(solution)/shard_map/ppermute | solution.py:24
  261.1 12.1 %collective-permute-done.29 = bf16[4,32,2048]{2,1,0:T(8,128)(2,1)S(1)} collective-permute-done((bf16[4,32,2048]{2,1,0:T(8,128)(2,1)S(1)}, bf16[4,32,2048]{2,1,0:T(8,128)(2,1)S(1)}, u32[]{:S(2)}, u32[]{:S(2)}) %collective-permute-start.29) | collective-permute-done | bytes 524320 | tf_op jit(solution)/shard_map/ppermute | solution.py:24
  279.7 4.3 %collective-permute-start.34 = (bf16[128,544]{1,0:T(8,128)(2,1)S(1)}, bf16[128,544]{1,0:T(8,128)(2,1)S(1)}, u32[]{:S(2)}, u32[]{:S(2)}) collective-permute-start(bf16[128,544]{1,0:T(8,128)(2,1)S(1)} %get-tuple-element.28), channel_id=1, source_target_pairs={{0,3},{1,0},{2,1},{3,2},{4,7},{5,4},{6,5},{7,6},{8,11},{9,8},{10,9... | collective-permute-start | bytes 417800 | tf_op jit(solution)/shard_map/ppermute | solution.py:24
  287.4 7.3 %collective-permute-done.33 = bf16[128,544]{1,0:T(8,128)(2,1)S(1)} collective-permute-done((bf16[128,544]{1,0:T(8,128)(2,1)S(1)}, bf16[128,544]{1,0:T(8,128)(2,1)S(1)}, u32[]{:S(2)}, u32[]{:S(2)}) %collective-permute-start.33) | collective-permute-done | bytes 139296 | tf_op jit(solution)/shard_map/ppermute | solution.py:24
  298.5 9.5 %local_scan.3 = (f32[2,1024,128]{2,1,0:T(8,128)S(1)}, f32[2,1024,128]{2,1,0:T(8,128)S(1)}, f32[17,16,128]{2,1,0:T(8,128)S(1)}) custom-call(f32[128,32]{1,0:T(8,128)S(1)} %slice.241.maps_ref, bf16[128,512]{1,0:T(8,128)(2,1)S(1)} %multiply_convert_fusion.rate_ref, bf16[512,2048]{1,0:T(8,128)(2,1)S(1)} %copy-done.2, f32[1,2048]{1,0:T(1,128)S(1)} %get-tuple-element.72.bias_ref, ...), custom_call_target="tpu_custom_call" | custom-call | tf_op jit(solution)/shard_map/local_scan/pallas_call | solution.py:159
  311.9 4.5 %collective-permute-done.36.rest_1_ = f32[17,16,128]{2,1,0:T(8,128)S(1)} collective-permute-done((f32[17,16,128]{2,1,0:T(8,128)S(1)}, f32[17,16,128]{2,1,0:T(8,128)S(1)}, u32[]{:S(2)}, u32[]{:S(2)}) %collective-permute-start.36) | collective-permute-done | bytes 139296 | tf_op jit(solution)/shard_map/ppermute | solution.py:29
  318.7 6.9 %finish_mixer.3 = bf16[128,2048]{1,0:T(8,128)(2,1)S(1)} custom-call(f32[128,32]{1,0:T(8,128)S(1)} %slice.241.maps_ref, f32[2,1024,128]{2,1,0:T(8,128)S(1)} %get-tuple-element.30.resp_ref, f32[2,1024,128]{2,1,0:T(8,128)S(1)} %get-tuple-element.31.cum_ref, f32[16,16,128]{2,1,0:T(8,128)S(1)} %bitcast.116, f32[1,2048]{1,0:T(1,128)S(1)} %get-tuple-element.71.skip_ref, ...), custom_call_target="tpu_custom_call" | custom-call | tf_op jit(solution)/shard_map/finish_mixer/pallas_call | solution.py:231
  327.8 11.3 %collective-permute-done.38 = bf16[128,2048]{1,0:T(8,128)(2,1)S(1)} collective-permute-done((bf16[128,2048]{1,0:T(8,128)(2,1)S(1)}, bf16[128,2048]{1,0:T(8,128)(2,1)S(1)}, u32[]{:S(2)}, u32[]{:S(2)}) %collective-permute-start.38) | collective-permute-done | bytes 524320 | tf_op jit(solution)/shard_map/ppermute | solution.py:386
  (171 shorter events, 110.0 us)
Async XLA Ops:
  1.4 25.6 %collective-permute-start.2 = (bf16[1024,544]{0,1:T(8,128)(2,1)S(1)}, bf16[1024,544]{0,1:T(8,128)(2,1)}, u32[]{:S(2)}, u32[]{:S(2)}) collective-permute-start(bf16[1024,544]{0,1:T(8,128)(2,1)S(1)} %dynamic-slice_bitcast_fusion), channel_id=1, source_target_pairs={{0,16},{16,0},{1,17},{17,1},{2,18},{18,2},{3,19},{19,3},{4,20},{20... | collective-permute-start | bytes 3342344 | tf_op jit(solution)/shard_map/ppermute | solution.py:33
  27.0 14.8 %collective-permute-start.3 = (bf16[1024,544]{0,1:T(8,128)(2,1)}, bf16[1024,544]{0,1:T(8,128)(2,1)}, u32[]{:S(2)}, u32[]{:S(2)}) collective-permute-start(bf16[1024,544]{0,1:T(8,128)(2,1)} %collective-permute-done.2), channel_id=1, source_target_pairs={{0,4},{4,0},{8,12},{12,8},{1,5},{5,1},{9,13},{13,9},{2,6},{6,2},{1... | collective-permute-start | bytes 3342344 | tf_op jit(solution)/shard_map/ppermute | solution.py:38
  28.6 18.1 %collective-permute-start = (bf16[16,2048]{1,0:T(8,128)(2,1)S(1)}, bf16[16,2048]{1,0:T(8,128)(2,1)S(1)}, u32[]{:S(2)}, u32[]{:S(2)}) collective-permute-start(bf16[16,2048]{1,0:T(8,128)(2,1)S(1)} %dynamic-slice_bitcast_fusion.11), channel_id=1, source_target_pairs={{0,4},{4,8},{8,12},{1,5},{5,9},{9,13},{2,6},{6,10},{10,14},{3,7},{... | collective-permute-start | bytes 196616 | tf_op jit(solution)/shard_map/ppermute | solution.py:29
  45.5 23.3 %collective-permute-start.7 = (bf16[256,2048]{1,0:T(8,128)(2,1)S(1)}, bf16[256,2048]{1,0:T(8,128)(2,1)S(1)}, u32[]{:S(2)}, u32[]{:S(2)}) collective-permute-start(bf16[256,2048]{1,0:T(8,128)(2,1)S(1)} %constant_dynamic-slice_fusion.5), channel_id=1, source_target_pairs={{0,16},{16,0},{1,17},{17,1},{2,18},{18,2},{3,19},{19,3},{4,20},{20... | collective-permute-start | bytes 3145736 | tf_op jit(solution)/shard_map/ppermute | solution.py:33
  49.0 22.8 %collective-permute-start.6 = (bf16[128,544]{1,0:T(8,128)(2,1)S(1)}, bf16[128,544]{1,0:T(8,128)(2,1)S(1)}, u32[]{:S(2)}, u32[]{:S(2)}) collective-permute-start(bf16[128,544]{1,0:T(8,128)(2,1)S(1)} %get-tuple-element.20), channel_id=1, source_target_pairs={{0,3},{1,0},{2,1},{3,2},{4,7},{5,4},{6,5},{7,6},{8,11},{9,8},{10,9... | collective-permute-start | bytes 417800 | tf_op jit(solution)/shard_map/ppermute | solution.py:24
  49.3 22.6 %collective-permute-start.5 = (bf16[128,544]{1,0:T(8,128)(2,1)S(1)}, bf16[128,544]{1,0:T(8,128)(2,1)S(1)}, u32[]{:S(2)}, u32[]{:S(2)}) collective-permute-start(bf16[128,544]{1,0:T(8,128)(2,1)S(1)} %get-tuple-element.20), channel_id=1, source_target_pairs={{0,2},{1,3},{2,0},{3,1},{4,6},{5,7},{6,4},{7,5},{8,10},{9,11},{10,... | collective-permute-start | bytes 417800 | tf_op jit(solution)/shard_map/ppermute | solution.py:24
  51.6 20.3 %collective-permute-start.4 = (bf16[128,544]{1,0:T(8,128)(2,1)S(1)}, bf16[128,544]{1,0:T(8,128)(2,1)S(1)}, u32[]{:S(2)}, u32[]{:S(2)}) collective-permute-start(bf16[128,544]{1,0:T(8,128)(2,1)S(1)} %get-tuple-element.20), channel_id=1, source_target_pairs={{0,1},{1,2},{2,3},{3,0},{4,5},{5,6},{6,7},{7,4},{8,9},{9,10},{10,1... | collective-permute-start | bytes 417800 | tf_op jit(solution)/shard_map/ppermute | solution.py:24
  74.6 15.2 %collective-permute-start.9 = (bf16[128,2048]{1,0:T(8,128)(2,1)S(1)}, bf16[128,2048]{1,0:T(8,128)(2,1)S(1)}, u32[]{:S(2)}, u32[]{:S(2)}) collective-permute-start(bf16[128,2048]{1,0:T(8,128)(2,1)S(1)} %copy-done.10), channel_id=1, source_target_pairs={{0,16},{16,0},{1,17},{17,1},{2,18},{18,2},{3,19},{19,3},{4,20},{20... | collective-permute-start | bytes 1572872 | tf_op jit(solution)/shard_map/ppermute | solution.py:33
  104.8 14.6 %collective-permute-start.18 = (bf16[128,2048]{1,0:T(8,128)(2,1)S(1)}, bf16[128,2048]{1,0:T(8,128)(2,1)}, u32[]{:S(2)}, u32[]{:S(2)}) collective-permute-start(bf16[128,2048]{1,0:T(8,128)(2,1)S(1)} %finish_mixer.2), channel_id=1, source_target_pairs={{0,12},{4,0},{8,4},{12,8},{1,13},{5,1},{9,5},{13,9},{2,14},{6,2},{... | collective-permute-start | bytes 1572872 | tf_op jit(solution)/shard_map/ppermute | solution.py:24
  104.9 14.5 %collective-permute-start.17 = (bf16[128,2048]{1,0:T(8,128)(2,1)S(1)}, bf16[128,2048]{1,0:T(8,128)(2,1)}, u32[]{:S(2)}, u32[]{:S(2)}) collective-permute-start(bf16[128,2048]{1,0:T(8,128)(2,1)S(1)} %finish_mixer.2), channel_id=1, source_target_pairs={{0,8},{4,12},{8,0},{12,4},{1,9},{5,13},{9,1},{13,5},{2,10},{6,14},... | collective-permute-start | bytes 1572872 | tf_op jit(solution)/shard_map/ppermute | solution.py:24
  104.9 22.9 %collective-permute-start.16 = (bf16[128,2048]{1,0:T(8,128)(2,1)S(1)}, bf16[128,2048]{1,0:T(8,128)(2,1)}, u32[]{:S(2)}, u32[]{:S(2)}) collective-permute-start(bf16[128,2048]{1,0:T(8,128)(2,1)S(1)} %finish_mixer.2), channel_id=1, source_target_pairs={{0,4},{4,8},{8,12},{12,0},{1,5},{5,9},{9,13},{13,1},{2,6},{6,10},{... | collective-permute-start | bytes 1572872 | tf_op jit(solution)/shard_map/ppermute | solution.py:24
  108.7 36.8 %collective-permute-start.15 = (bf16[32,2048]{1,0:T(8,128)(2,1)}, bf16[32,2048]{1,0:T(8,128)(2,1)}, u32[]{:S(2)}, u32[]{:S(2)}) collective-permute-start(bf16[32,2048]{1,0:T(8,128)(2,1)} %get-tuple-element.51), channel_id=1, source_target_pairs={{0,12},{4,0},{8,4},{12,8},{1,13},{5,1},{9,5},{13,9},{2,14},{6,2},{... | collective-permute-start | bytes 393224 | tf_op jit(solution)/shard_map/ppermute | solution.py:24
  136.5 16.8 %collective-permute-start.21 = (bf16[128,2048]{1,0:T(8,128)(2,1)}, bf16[128,2048]{1,0:T(8,128)(2,1)}, u32[]{:S(2)}, u32[]{:S(2)}) collective-permute-start(bf16[128,2048]{1,0:T(8,128)(2,1)} %convolution_convert_fusion), channel_id=1, source_target_pairs={{0,1},{1,2},{2,3},{3,0},{4,5},{5,6},{6,7},{7,4},{8,9},{9,10},{10,1... | collective-permute-start | bytes 1572872 | tf_op jit(solution)/shard_map/ppermute | solution.py:24
  139.9 40.4 %collective-permute-start.20 = (bf16[128,2048]{1,0:T(8,128)(2,1)}, bf16[128,2048]{1,0:T(8,128)(2,1)}, u32[]{:S(2)}, u32[]{:S(2)}) collective-permute-start(bf16[128,2048]{1,0:T(8,128)(2,1)} %convolution_convert_fusion.1), channel_id=1, source_target_pairs={{0,2},{1,3},{2,0},{3,1},{4,6},{5,7},{6,4},{7,5},{8,10},{9,11},{10,... | collective-permute-start | bytes 1572872 | tf_op jit(solution)/shard_map/ppermute | solution.py:24
  143.0 42.2 %collective-permute-start.19 = (bf16[128,2048]{1,0:T(8,128)(2,1)}, bf16[128,2048]{1,0:T(8,128)(2,1)}, u32[]{:S(2)}, u32[]{:S(2)}) collective-permute-start(bf16[128,2048]{1,0:T(8,128)(2,1)} %convolution_convert_fusion.2), channel_id=1, source_target_pairs={{0,3},{1,0},{2,1},{3,2},{4,7},{5,4},{6,5},{7,6},{8,11},{9,8},{10,9... | collective-permute-start | bytes 1572872 | tf_op jit(solution)/shard_map/ppermute | solution.py:24
  197.9 13.5 %collective-permute-start.27 = (bf16[128,2048]{1,0:T(8,128)(2,1)S(1)}, bf16[128,2048]{1,0:T(8,128)(2,1)S(1)}, u32[]{:S(2)}, u32[]{:S(2)}) collective-permute-start(bf16[128,2048]{1,0:T(8,128)(2,1)S(1)} %fusion.2), channel_id=1, source_target_pairs={{0,3},{1,0},{2,1},{3,2},{4,7},{5,4},{6,5},{7,6},{8,11},{9,8},{10,9... | collective-permute-start | bytes 1572872 | tf_op jit(solution)/shard_map/ppermute | solution.py:24
  198.0 33.8 %collective-permute-start.26 = (bf16[128,2048]{1,0:T(8,128)(2,1)S(1)}, bf16[128,2048]{1,0:T(8,128)(2,1)S(1)}, u32[]{:S(2)}, u32[]{:S(2)}) collective-permute-start(bf16[128,2048]{1,0:T(8,128)(2,1)S(1)} %fusion.2), channel_id=1, source_target_pairs={{0,2},{1,3},{2,0},{3,1},{4,6},{5,7},{6,4},{7,5},{8,10},{9,11},{10,... | collective-permute-start | bytes 1572872 | tf_op jit(solution)/shard_map/ppermute | solution.py:24
  198.5 44.5 %collective-permute-start.25 = (bf16[128,2048]{1,0:T(8,128)(2,1)S(1)}, bf16[128,2048]{1,0:T(8,128)(2,1)S(1)}, u32[]{:S(2)}, u32[]{:S(2)}) collective-permute-start(bf16[128,2048]{1,0:T(8,128)(2,1)S(1)} %fusion.2), channel_id=1, source_target_pairs={{0,1},{1,2},{2,3},{3,0},{4,5},{5,6},{6,7},{7,4},{8,9},{9,10},{10,1... | collective-permute-start | bytes 1572872 | tf_op jit(solution)/shard_map/ppermute | solution.py:24
  246.0 15.1 %collective-permute-start.30 = (bf16[4,32,2048]{2,1,0:T(8,128)(2,1)S(1)}, bf16[4,32,2048]{2,1,0:T(8,128)(2,1)S(1)}, u32[]{:S(2)}, u32[]{:S(2)}) collective-permute-start(bf16[4,32,2048]{2,1,0:T(8,128)(2,1)S(1)} %pad_maximum_fusion.6), channel_id=1, source_target_pairs={{0,4},{4,8},{8,12},{12,0},{1,5},{5,9},{9,13},{13,1},{2,6},{6,10},{... | collective-permute-start | bytes 1572872 | tf_op jit(solution)/shard_map/ppermute | solution.py:24
  250.1 23.0 %collective-permute-start.29 = (bf16[4,32,2048]{2,1,0:T(8,128)(2,1)S(1)}, bf16[4,32,2048]{2,1,0:T(8,128)(2,1)S(1)}, u32[]{:S(2)}, u32[]{:S(2)}) collective-permute-start(bf16[4,32,2048]{2,1,0:T(8,128)(2,1)S(1)} %pad_maximum_fusion.5), channel_id=1, source_target_pairs={{0,8},{4,12},{8,0},{12,4},{1,9},{5,13},{9,1},{13,5},{2,10},{6,14},... | collective-permute-start | bytes 1572872 | tf_op jit(solution)/shard_map/ppermute | solution.py:24
  250.6 23.2 %collective-permute-start.28 = (bf16[4,32,2048]{2,1,0:T(8,128)(2,1)S(1)}, bf16[4,32,2048]{2,1,0:T(8,128)(2,1)S(1)}, u32[]{:S(2)}, u32[]{:S(2)}) collective-permute-start(bf16[4,32,2048]{2,1,0:T(8,128)(2,1)S(1)} %pad_maximum_fusion.4), channel_id=1, source_target_pairs={{0,12},{4,0},{8,4},{12,8},{1,13},{5,1},{9,5},{13,9},{2,14},{6,2},{... | collective-permute-start | bytes 1572872 | tf_op jit(solution)/shard_map/ppermute | solution.py:24
  284.0 14.2 %collective-permute-start.32 = (bf16[128,544]{1,0:T(8,128)(2,1)S(1)}, bf16[128,544]{1,0:T(8,128)(2,1)S(1)}, u32[]{:S(2)}, u32[]{:S(2)}) collective-permute-start(bf16[128,544]{1,0:T(8,128)(2,1)S(1)} %get-tuple-element.28), channel_id=1, source_target_pairs={{0,1},{1,2},{2,3},{3,0},{4,5},{5,6},{6,7},{7,4},{8,9},{9,10},{10,1... | collective-permute-start | bytes 417800 | tf_op jit(solution)/shard_map/ppermute | solution.py:24
  285.3 42.5 %collective-permute-start.39 = (bf16[128,2048]{1,0:T(8,128)(2,1)S(1)}, bf16[128,2048]{1,0:T(8,128)(2,1)S(1)}, u32[]{:S(2)}, u32[]{:S(2)}) collective-permute-start(bf16[128,2048]{1,0:T(8,128)(2,1)S(1)} %finish_mixer.2), channel_id=1, source_target_pairs={{16,0},{17,1},{18,2},{19,3},{20,4},{21,5},{22,6},{23,7},{24,8},{25... | collective-permute-start | bytes 1572872 | tf_op jit(solution)/shard_map/ppermute | solution.py:333
  325.5 13.6 %collective-permute-start.38 = (bf16[128,2048]{1,0:T(8,128)(2,1)S(1)}, bf16[128,2048]{1,0:T(8,128)(2,1)S(1)}, u32[]{:S(2)}, u32[]{:S(2)}) collective-permute-start(bf16[128,2048]{1,0:T(8,128)(2,1)S(1)} %finish_mixer.3), channel_id=1, source_target_pairs={{0,16},{1,17},{2,18},{3,19},{4,20},{5,21},{6,22},{7,23},{8,24},{9,... | collective-permute-start | bytes 1572872 | tf_op jit(solution)/shard_map/ppermute | solution.py:386
  (33 other events, 325.4 us)

commit v2 on v1

--- a/solution.py
+++ b/solution.py
@@ -334,15 +334,20 @@
 
     hidden = lax.dynamic_index_in_dim(hidden_in, segment, 0, False)
     hidden_parts = []
-    for s in range(ctx):
+    for s in range(0, ctx, 2):
         target = lax.rem(place + s, ctx)
         piece = lax.dynamic_slice_in_dim(hidden, target * depth, depth, 1)
         hidden_parts.append(piece if s == 0 else rotated(piece, "ctx", s))
+        piece = lax.dynamic_slice_in_dim(hidden, (target ^ 1) * depth, depth, 1)
+        route = [(i, ((i + s) % ctx) ^ 1) for i in range(ctx)]
+        hidden_parts.append(lax.ppermute(piece, "ctx", route))
     hidden_rows = jnp.stack(hidden_parts, axis=0)
 
-    every = jnp.stack(
-        [mixed_first] + [rotated(mixed_first, "ctx", s) for s in range(1, ctx)], axis=0
-    ).reshape(ctx, tp, block, width)
+    fetched = []
+    for s in range(0, ctx, 2):
+        part = mixed_first if s == 0 else rotated(mixed_first, "ctx", s)
+        fetched += [part, sibling(part)]
+    every = jnp.stack(fetched, axis=0).reshape(ctx, tp, block, width)
     link = None
     for s in reversed(range(tp)):
         target = lax.rem(column + s, tp)
@@ -352,12 +357,16 @@
         link = part.astype(F32) if link is None else link + part.astype(F32)
     carried = (hidden_rows.reshape(ctx * block, depth).astype(F32) + link).astype(BF16)
     wide = carried.astype(F32)
-    order = lax.rem(place - jnp.arange(ctx) + ctx, ctx)
-    square = jnp.sum(wide * wide, axis=1).reshape(ctx, block)[order]
+    index = jnp.arange(ctx)
+    odd = index % 2
+    holder = lax.rem((place ^ odd) - (index - odd) + ctx, ctx)
+    apart = (index ^ place) & 1
+    slot = lax.rem((place ^ apart) - index + ctx, ctx) + apart
+    square = jnp.sum(wide * wide, axis=1).reshape(ctx, block)[slot]
     squares = square
     for s in range(1, ctx):
         squares = squares + rotated(square, "ctx", s)
-    scale = lax.rsqrt(squares[order].reshape(-1, 1) / (depth * ctx) + 1e-05)
+    scale = lax.rsqrt(squares[holder].reshape(-1, 1) / (depth * ctx) + 1e-05)
     gain = lax.dynamic_slice_in_dim(norm_gain, place * depth, depth, 0)
     normed = (wide * scale * gain[None, :]).astype(BF16)
 
@@ -370,8 +379,10 @@
             ).reshape(ctx, block, width)
         )
     made = None
-    for s in range(ctx):
+    for s in reversed(range(0, ctx, 2)):
         rows = jnp.stack([product[s] for product in products], axis=0)
+        others = jnp.stack([product[s + 1] for product in products], axis=0)
+        rows = rows + sibling(others.astype(BF16)).astype(F32)
         part = rows if s == 0 else rotated(rows.astype(BF16), "ctx", -s)
         made = part.astype(F32) if made is None else made + part.astype(F32)
     made = made.astype(BF16)

time: 343 us -> 325 us (0.948)
  waiting for transfers between devices: 182 us -> 168 us
  matrix products: 34.9 us -> 28.6 us
  starting transfers between devices: 53 us -> 48.8 us
  local copies, waits for them, and re-layouts: 20.2 us -> 23.9 us
    ppermute x24 -> x18, waiting for transfers between devices: 115 us -> 98.9 us  [rotated(): lax.ppermute(block, axis, [(i, (i + distance) % count) for i in range(cou...]
    ppermute x24 -> x18, starting transfers between devices: 32 us -> 20.7 us  [rotated(): lax.ppermute(block, axis, [(i, (i + distance) % count) for i in range(cou...]
    dot_general x4, matrix products: 16.4 us -> 10.1 us  [shards(): product = jnp.dot(rows, out_proj, preferred_element_type=F32)]
    ppermute x2 -> x6, starting transfers between devices: 3.88 us -> 8.91 us  [sibling(): return lax.ppermute(block, 'ctx', [(i, i ^ 1) for i in range(count)])]
    unnamed x35 -> x37, local copies, waits for them, and re-layouts: 7.07 us -> 7.05 us
  transfers between devices with their start and end apart: 40 -> 40, of which waited for: 24 -> 21; matrix products, arithmetic and copies ran while one was open for 14% -> 16% of each run, Pallas kernels for 8% -> 9%
where the time goes in v2:
time: 325 us; the launch traced here: 322 us
  waiting for transfers between devices  168 us (52%)
  starting transfers between devices  48.8 us (15%)
  Pallas kernels  37.4 us (12%)
  matrix products  28.6 us (9%)
  local copies, waits for them, and re-layouts  23.9 us (7%)
  other arithmetic  14.7 us (5%)
    ppermute x18, waiting for transfers between devices, rotated(): lax.ppermute(block, axis, [(i, (i + distance) % count) for i in range(cou...  98.9 us
    ppermute x4, waiting for transfers between devices, swapped(): return lax.ppermute(block, 'pipe', [(0, 1), (1, 0)])  39.3 us
    ppermute x18, starting transfers between devices, rotated(): lax.ppermute(block, axis, [(i, (i + distance) % count) for i in range(cou...  20.7 us
    pallas_call x2, Pallas kernels, local_scan(): pl.pallas_call(functools.partial(scan_kernel, nstate), grid=(tiles,), in_...  19 us
    dot_general x4, matrix products, shards(): lax.dot_general(part, in_proj, (((1,), (1,)), ((), ())), preferred_elemen...  18.5 us
    ppermute x8, waiting for transfers between devices, shifted(): lax.ppermute(block, axis, [(i - distance, i) for i in range(distance, cou...  16.4 us
    pallas_call x2, Pallas kernels, finish(): pl.pallas_call(functools.partial(finish_kernel, nstate, len(ends)), grid=...  13.7 us
    ppermute x1, waiting for transfers between devices, shards(): kept_second = lax.ppermute(mixed_second, 'pipe', [(0, 1)])  11.3 us
  transfers between devices with their start and end apart: 40, of which 21 were waited for; matrix products, arithmetic and copies ran while one was open for 16% of the time, Pallas kernels for 9%

profile of v2, /device:TPU:11, one launch (start us, length us, event | category | flops | bytes accessed | tf_op | source)
XLA Modules:
  0.0 322.1 jit_solution(7018513323040001132)
XLA Ops:
  2.7 24.3 %collective-permute-done.2 = bf16[1024,544]{0,1:T(8,128)(2,1)} collective-permute-done((bf16[1024,544]{0,1:T(8,128)(2,1)S(1)}, bf16[1024,544]{0,1:T(8,128)(2,1)}, u32[]{:S(2)}, u32[]{:S(2)}) %collective-permute-start.2) | collective-permute-done | bytes 1114144 | tf_op jit(solution)/shard_map/ppermute | solution.py:33
  33.8 4.4 %copy.16 = bf16[1,2048,544]{2,1,0:T(8,128)(2,1)} copy(bf16[1,2048,544]{1,2,0:T(8,128)(2,1)} %param.21) | data formatting | bytes 4456448 | tf_op args[8]
  53.8 15.0 %collective-permute-done.7 = bf16[256,2048]{1,0:T(8,128)(2,1)S(1)} collective-permute-done((bf16[256,2048]{1,0:T(8,128)(2,1)S(1)}, bf16[256,2048]{1,0:T(8,128)(2,1)S(1)}, u32[]{:S(2)}, u32[]{:S(2)}) %collective-permute-start.7) | collective-permute-done | bytes 1048608 | tf_op jit(solution)/shard_map/ppermute | solution.py:33
  76.4 9.5 %local_scan.2 = (f32[2,1024,128]{2,1,0:T(8,128)S(1)}, f32[2,1024,128]{2,1,0:T(8,128)S(1)}, f32[17,16,128]{2,1,0:T(8,128)S(1)}) custom-call(f32[128,32]{1,0:T(8,128)S(1)} %slice.214.maps_ref, bf16[128,512]{1,0:T(8,128)(2,1)S(1)} %multiply_convert_fusion.1.rate_ref, bf16[512,2048]{1,0:T(8,128)(2,1)S(1)} %get-tuple-element.38.dt_ref, ...), custom_call_target="tpu_custom_call" | custom-call | tf_op jit(solution)/shard_map/local_scan/pallas_call | solution.py:159
  90.8 5.5 %collective-permute-done.11.rest_1_ = f32[17,16,128]{2,1,0:T(8,128)S(1)} collective-permute-done((f32[17,16,128]{2,1,0:T(8,128)S(1)}, f32[17,16,128]{2,1,0:T(8,128)S(1)}, u32[]{:S(2)}, u32[]{:S(2)}) %collective-permute-start.11) | collective-permute-done | bytes 139296 | tf_op jit(solution)/shard_map/ppermute | solution.py:29
  98.0 6.9 %finish_mixer.2 = bf16[128,2048]{1,0:T(8,128)(2,1)S(1)} custom-call(f32[128,32]{1,0:T(8,128)S(1)} %slice.214.maps_ref, f32[2,1024,128]{2,1,0:T(8,128)S(1)} %get-tuple-element.24.resp_ref, f32[2,1024,128]{2,1,0:T(8,128)S(1)} %get-tuple-element.25.cum_ref, f32[16,16,128]{2,1,0:T(8,128)S(1)} %bitcast.116, f32[1,2048]{1,0:T(1,128)S(1)} %get-tuple-element.78.skip_ref, ...), custom_call_target="tpu_custom_call" | custom-call | tf_op jit(solution)/shard_map/finish_mixer/pallas_call | solution.py:231
  105.2 13.2 %collective-permute-done.17 = bf16[128,2048]{1,0:T(8,128)(2,1)} collective-permute-done((bf16[128,2048]{1,0:T(8,128)(2,1)S(1)}, bf16[128,2048]{1,0:T(8,128)(2,1)}, u32[]{:S(2)}, u32[]{:S(2)}) %collective-permute-start.17) | collective-permute-done | bytes 524320 | tf_op jit(solution)/shard_map/ppermute | solution.py:24
  124.1 4.8 %convolution_convert_fusion = bf16[128,2048]{1,0:T(8,128)(2,1)S(1)} fusion(bf16[128,2048]{1,0:T(8,128)(2,1)S(1)} %bitcast.126, bf16[2048,2048]{1,0:T(8,128)(2,1)} %param.16), kind=kOutput, calls=%fused_computation.5 | convolution fusion | flops 1074003968 | bytes 9437184 | tf_op jit(solution)/shard_map/dot_general | solution.py:355
  141.8 32.8 %collective-permute-done.20 = bf16[128,2048]{1,0:T(8,128)(2,1)S(1)} collective-permute-done((bf16[128,2048]{1,0:T(8,128)(2,1)S(1)}, bf16[128,2048]{1,0:T(8,128)(2,1)S(1)}, u32[]{:S(2)}, u32[]{:S(2)}) %collective-permute-start.20) | collective-permute-done | bytes 524320 | tf_op jit(solution)/shard_map/ppermute | solution.py:24
  189.3 6.4 %fusion.20 = (bf16[128,2048]{1,0:T(8,128)(2,1)S(1)}, f32[128,2048]{1,0:T(8,128)S(1)}) fusion(bf16[128,2048]{1,0:T(8,128)(2,1)S(1)} %fusion.2, bf16[2048,2048]{1,0:T(8,128)(2,1)} %param.17), kind=kOutput, calls=%fused_computation.106 | convolution fusion | flops 1074003968 | bytes 10485760 | tf_op jit(solution)/shard_map/dot_general | solution.py:377
  197.5 6.3 %fusion.17 = (bf16[128,2048]{1,0:T(8,128)(2,1)S(1)}, f32[128,2048]{1,0:T(8,128)S(1)}) fusion(bf16[128,2048]{1,0:T(8,128)(2,1)S(1)} %collective-permute-done.27, bf16[2048,2048]{1,0:T(8,128)(2,1)} %param.17), kind=kOutput, calls=%fused_computation.103 | convolution fusion | flops 1074003968 | bytes 10485760 | tf_op jit(solution)/shard_map/dot_general | solution.py:377
  204.5 15.7 %collective-permute-done.26 = bf16[128,2048]{1,0:T(8,128)(2,1)S(1)} collective-permute-done((bf16[128,2048]{1,0:T(8,128)(2,1)S(1)}, bf16[128,2048]{1,0:T(8,128)(2,1)S(1)}, u32[]{:S(2)}, u32[]{:S(2)}) %collective-permute-start.26) | collective-permute-done | bytes 524320 | tf_op jit(solution)/shard_map/ppermute | solution.py:24
  220.3 2.9 fusion.18
  223.9 7.6 %collective-permute-done.25 = bf16[128,2048]{1,0:T(8,128)(2,1)S(1)} collective-permute-done((bf16[128,2048]{1,0:T(8,128)(2,1)S(1)}, bf16[128,2048]{1,0:T(8,128)(2,1)S(1)}, u32[]{:S(2)}, u32[]{:S(2)}) %collective-permute-start.25) | collective-permute-done | bytes 524320 | tf_op jit(solution)/shard_map/ppermute | solution.py:24
  231.5 2.9 fusion.19
  234.5 4.4 %collective-permute-start.28 = (bf16[4,32,2048]{2,1,0:T(8,128)(2,1)S(1)}, bf16[4,32,2048]{2,1,0:T(8,128)(2,1)S(1)}, u32[]{:S(2)}, u32[]{:S(2)}) collective-permute-start(bf16[4,32,2048]{2,1,0:T(8,128)(2,1)S(1)} %pad_maximum_fusion.4), channel_id=1, source_target_pairs={{0,4},{4,0},{8,12},{12,8},{1,5},{5,1},{9,13},{13,9},{2,6},{6,2},{1... | collective-permute-start | bytes 1572872 | tf_op jit(solution)/shard_map/ppermute | solution.py:38
  243.8 11.0 %collective-permute-done.29 = bf16[4,32,2048]{2,1,0:T(8,128)(2,1)} collective-permute-done((bf16[4,32,2048]{2,1,0:T(8,128)(2,1)}, bf16[4,32,2048]{2,1,0:T(8,128)(2,1)}, u32[]{:S(2)}, u32[]{:S(2)}) %collective-permute-start.29) | collective-permute-done | bytes 524320 | tf_op jit(solution)/shard_map/ppermute | solution.py:24
  262.9 3.0 collective-permute-start.34
  269.0 7.5 %collective-permute-done.33 = bf16[128,544]{1,0:T(8,128)(2,1)S(1)} collective-permute-done((bf16[128,544]{1,0:T(8,128)(2,1)S(1)}, bf16[128,544]{1,0:T(8,128)(2,1)S(1)}, u32[]{:S(2)}, u32[]{:S(2)}) %collective-permute-start.33) | collective-permute-done | bytes 139296 | tf_op jit(solution)/shard_map/ppermute | solution.py:24
  276.5 3.5 %collective-permute-done.32 = bf16[128,544]{1,0:T(8,128)(2,1)S(1)} collective-permute-done((bf16[128,544]{1,0:T(8,128)(2,1)S(1)}, bf16[128,544]{1,0:T(8,128)(2,1)S(1)}, u32[]{:S(2)}, u32[]{:S(2)}) %collective-permute-start.32) | collective-permute-done | bytes 139296 | tf_op jit(solution)/shard_map/ppermute | solution.py:24
  280.4 9.5 %local_scan.3 = (f32[2,1024,128]{2,1,0:T(8,128)S(1)}, f32[2,1024,128]{2,1,0:T(8,128)S(1)}, f32[17,16,128]{2,1,0:T(8,128)S(1)}) custom-call(f32[128,32]{1,0:T(8,128)S(1)} %slice.237.maps_ref, bf16[128,512]{1,0:T(8,128)(2,1)S(1)} %multiply_convert_fusion.rate_ref, bf16[512,2048]{1,0:T(8,128)(2,1)S(1)} %copy-done.2, f32[1,2048]{1,0:T(1,128)S(1)} %get-tuple-element.76.bias_ref, ...), custom_call_target="tpu_custom_call" | custom-call | tf_op jit(solution)/shard_map/local_scan/pallas_call | solution.py:159
  293.8 4.5 %collective-permute-done.36.rest_1_ = f32[17,16,128]{2,1,0:T(8,128)S(1)} collective-permute-done((f32[17,16,128]{2,1,0:T(8,128)S(1)}, f32[17,16,128]{2,1,0:T(8,128)S(1)}, u32[]{:S(2)}, u32[]{:S(2)}) %collective-permute-start.36) | collective-permute-done | bytes 139296 | tf_op jit(solution)/shard_map/ppermute | solution.py:29
  300.6 6.9 %finish_mixer.3 = bf16[128,2048]{1,0:T(8,128)(2,1)S(1)} custom-call(f32[128,32]{1,0:T(8,128)S(1)} %slice.237.maps_ref, f32[2,1024,128]{2,1,0:T(8,128)S(1)} %get-tuple-element.30.resp_ref, f32[2,1024,128]{2,1,0:T(8,128)S(1)} %get-tuple-element.31.cum_ref, f32[16,16,128]{2,1,0:T(8,128)S(1)} %bitcast.118, f32[1,2048]{1,0:T(1,128)S(1)} %get-tuple-element.75.skip_ref, ...), custom_call_target="tpu_custom_call" | custom-call | tf_op jit(solution)/shard_map/finish_mixer/pallas_call | solution.py:231
  309.7 11.3 %collective-permute-done.38 = bf16[128,2048]{1,0:T(8,128)(2,1)S(1)} collective-permute-done((bf16[128,2048]{1,0:T(8,128)(2,1)S(1)}, bf16[128,2048]{1,0:T(8,128)(2,1)S(1)}, u32[]{:S(2)}, u32[]{:S(2)}) %collective-permute-start.38) | collective-permute-done | bytes 524320 | tf_op jit(solution)/shard_map/ppermute | solution.py:397
  (174 shorter events, 101.6 us)
Async XLA Ops:
  1.4 25.6 %collective-permute-start.2 = (bf16[1024,544]{0,1:T(8,128)(2,1)S(1)}, bf16[1024,544]{0,1:T(8,128)(2,1)}, u32[]{:S(2)}, u32[]{:S(2)}) collective-permute-start(bf16[1024,544]{0,1:T(8,128)(2,1)S(1)} %dynamic-slice_bitcast_fusion), channel_id=1, source_target_pairs={{0,16},{16,0},{1,17},{17,1},{2,18},{18,2},{3,19},{19,3},{4,20},{20... | collective-permute-start | bytes 3342344 | tf_op jit(solution)/shard_map/ppermute | solution.py:33
  27.0 14.8 %collective-permute-start.3 = (bf16[1024,544]{0,1:T(8,128)(2,1)}, bf16[1024,544]{0,1:T(8,128)(2,1)}, u32[]{:S(2)}, u32[]{:S(2)}) collective-permute-start(bf16[1024,544]{0,1:T(8,128)(2,1)} %collective-permute-done.2), channel_id=1, source_target_pairs={{0,4},{4,0},{8,12},{12,8},{1,5},{5,1},{9,13},{13,9},{2,6},{6,2},{1... | collective-permute-start | bytes 3342344 | tf_op jit(solution)/shard_map/ppermute | solution.py:38
  28.6 18.2 %collective-permute-start = (bf16[16,2048]{1,0:T(8,128)(2,1)S(1)}, bf16[16,2048]{1,0:T(8,128)(2,1)S(1)}, u32[]{:S(2)}, u32[]{:S(2)}) collective-permute-start(bf16[16,2048]{1,0:T(8,128)(2,1)S(1)} %dynamic-slice_bitcast_fusion.11), channel_id=1, source_target_pairs={{0,4},{4,8},{8,12},{1,5},{5,9},{9,13},{2,6},{6,10},{10,14},{3,7},{... | collective-permute-start | bytes 196616 | tf_op jit(solution)/shard_map/ppermute | solution.py:29
  45.5 23.3 %collective-permute-start.7 = (bf16[256,2048]{1,0:T(8,128)(2,1)S(1)}, bf16[256,2048]{1,0:T(8,128)(2,1)S(1)}, u32[]{:S(2)}, u32[]{:S(2)}) collective-permute-start(bf16[256,2048]{1,0:T(8,128)(2,1)S(1)} %constant_dynamic-slice_fusion.5), channel_id=1, source_target_pairs={{0,16},{16,0},{1,17},{17,1},{2,18},{18,2},{3,19},{19,3},{4,20},{20... | collective-permute-start | bytes 3145736 | tf_op jit(solution)/shard_map/ppermute | solution.py:33
  49.1 22.8 %collective-permute-start.6 = (bf16[128,544]{1,0:T(8,128)(2,1)S(1)}, bf16[128,544]{1,0:T(8,128)(2,1)S(1)}, u32[]{:S(2)}, u32[]{:S(2)}) collective-permute-start(bf16[128,544]{1,0:T(8,128)(2,1)S(1)} %get-tuple-element.20), channel_id=1, source_target_pairs={{0,3},{1,0},{2,1},{3,2},{4,7},{5,4},{6,5},{7,6},{8,11},{9,8},{10,9... | collective-permute-start | bytes 417800 | tf_op jit(solution)/shard_map/ppermute | solution.py:24
  49.3 22.6 %collective-permute-start.5 = (bf16[128,544]{1,0:T(8,128)(2,1)S(1)}, bf16[128,544]{1,0:T(8,128)(2,1)S(1)}, u32[]{:S(2)}, u32[]{:S(2)}) collective-permute-start(bf16[128,544]{1,0:T(8,128)(2,1)S(1)} %get-tuple-element.20), channel_id=1, source_target_pairs={{0,2},{1,3},{2,0},{3,1},{4,6},{5,7},{6,4},{7,5},{8,10},{9,11},{10,... | collective-permute-start | bytes 417800 | tf_op jit(solution)/shard_map/ppermute | solution.py:24
  51.6 20.3 %collective-permute-start.4 = (bf16[128,544]{1,0:T(8,128)(2,1)S(1)}, bf16[128,544]{1,0:T(8,128)(2,1)S(1)}, u32[]{:S(2)}, u32[]{:S(2)}) collective-permute-start(bf16[128,544]{1,0:T(8,128)(2,1)S(1)} %get-tuple-element.20), channel_id=1, source_target_pairs={{0,1},{1,2},{2,3},{3,0},{4,5},{5,6},{6,7},{7,4},{8,9},{9,10},{10,1... | collective-permute-start | bytes 417800 | tf_op jit(solution)/shard_map/ppermute | solution.py:24
  74.6 15.2 %collective-permute-start.9 = (bf16[128,2048]{1,0:T(8,128)(2,1)S(1)}, bf16[128,2048]{1,0:T(8,128)(2,1)S(1)}, u32[]{:S(2)}, u32[]{:S(2)}) collective-permute-start(bf16[128,2048]{1,0:T(8,128)(2,1)S(1)} %copy-done.11), channel_id=1, source_target_pairs={{0,16},{16,0},{1,17},{17,1},{2,18},{18,2},{3,19},{19,3},{4,20},{20... | collective-permute-start | bytes 1572872 | tf_op jit(solution)/shard_map/ppermute | solution.py:33
  88.6 9.4 %collective-permute-start.12 = (f32[17,16,128]{2,1,0:T(8,128)S(1)}, f32[17,16,128]{2,1,0:T(8,128)S(1)}, u32[]{:S(2)}, u32[]{:S(2)}) collective-permute-start(f32[17,16,128]{2,1,0:T(8,128)S(1)} %get-tuple-element.27), channel_id=1, source_target_pairs={{0,12},{1,13},{2,14},{3,15},{16,28},{17,29},{18,30},{19,31}} | collective-permute-start | bytes 417800 | tf_op jit(solution)/shard_map/ppermute | solution.py:29
  104.9 13.5 %collective-permute-start.17 = (bf16[128,2048]{1,0:T(8,128)(2,1)S(1)}, bf16[128,2048]{1,0:T(8,128)(2,1)}, u32[]{:S(2)}, u32[]{:S(2)}) collective-permute-start(bf16[128,2048]{1,0:T(8,128)(2,1)S(1)} %finish_mixer.2), channel_id=1, source_target_pairs={{0,8},{4,12},{8,0},{12,4},{1,9},{5,13},{9,1},{13,5},{2,10},{6,14},... | collective-permute-start | bytes 1572872 | tf_op jit(solution)/shard_map/ppermute | solution.py:24
  104.9 17.2 %collective-permute-start.16 = (bf16[128,2048]{1,0:T(8,128)(2,1)S(1)}, bf16[128,2048]{1,0:T(8,128)(2,1)}, u32[]{:S(2)}, u32[]{:S(2)}) collective-permute-start(bf16[128,2048]{1,0:T(8,128)(2,1)S(1)} %finish_mixer.2), channel_id=1, source_target_pairs={{0,4},{4,0},{8,12},{12,8},{1,5},{5,1},{9,13},{13,9},{2,6},{6,2},{1... | collective-permute-start | bytes 1572872 | tf_op jit(solution)/shard_map/ppermute | solution.py:38
  120.6 15.1 %collective-permute-start.15 = (bf16[32,2048]{1,0:T(8,128)(2,1)}, bf16[32,2048]{1,0:T(8,128)(2,1)}, u32[]{:S(2)}, u32[]{:S(2)}) collective-permute-start(bf16[32,2048]{1,0:T(8,128)(2,1)} %get-tuple-element.59), channel_id=1, source_target_pairs={{0,12},{4,8},{8,4},{12,0},{1,13},{5,9},{9,5},{13,1},{2,14},{6,10},... | collective-permute-start | bytes 393224 | tf_op jit(solution)/shard_map/ppermute | solution.py:343
  121.2 16.0 %collective-permute-start.14 = (bf16[32,2048]{1,0:T(8,128)(2,1)S(1)}, bf16[32,2048]{1,0:T(8,128)(2,1)}, u32[]{:S(2)}, u32[]{:S(2)}) collective-permute-start(bf16[32,2048]{1,0:T(8,128)(2,1)S(1)} %get-tuple-element.60), channel_id=1, source_target_pairs={{0,8},{4,12},{8,0},{12,4},{1,9},{5,13},{9,1},{13,5},{2,10},{6,14},... | collective-permute-start | bytes 393224 | tf_op jit(solution)/shard_map/ppermute | solution.py:24
  128.9 12.9 %collective-permute-start.21 = (bf16[128,2048]{1,0:T(8,128)(2,1)S(1)}, bf16[128,2048]{1,0:T(8,128)(2,1)S(1)}, u32[]{:S(2)}, u32[]{:S(2)}) collective-permute-start(bf16[128,2048]{1,0:T(8,128)(2,1)S(1)} %convolution_convert_fusion), channel_id=1, source_target_pairs={{0,1},{1,2},{2,3},{3,0},{4,5},{5,6},{6,7},{7,4},{8,9},{9,10},{10,1... | collective-permute-start | bytes 1572872 | tf_op jit(solution)/shard_map/ppermute | solution.py:24
  131.6 43.0 %collective-permute-start.20 = (bf16[128,2048]{1,0:T(8,128)(2,1)S(1)}, bf16[128,2048]{1,0:T(8,128)(2,1)S(1)}, u32[]{:S(2)}, u32[]{:S(2)}) collective-permute-start(bf16[128,2048]{1,0:T(8,128)(2,1)S(1)} %convolution_convert_fusion.1), channel_id=1, source_target_pairs={{0,2},{1,3},{2,0},{3,1},{4,6},{5,7},{6,4},{7,5},{8,10},{9,11},{10,... | collective-permute-start | bytes 1572872 | tf_op jit(solution)/shard_map/ppermute | solution.py:24
  134.7 42.6 %collective-permute-start.19 = (bf16[128,2048]{1,0:T(8,128)(2,1)S(1)}, bf16[128,2048]{1,0:T(8,128)(2,1)S(1)}, u32[]{:S(2)}, u32[]{:S(2)}) collective-permute-start(bf16[128,2048]{1,0:T(8,128)(2,1)S(1)} %convolution_convert_fusion.2), channel_id=1, source_target_pairs={{0,3},{1,0},{2,1},{3,2},{4,7},{5,4},{6,5},{7,6},{8,11},{9,8},{10,9... | collective-permute-start | bytes 1572872 | tf_op jit(solution)/shard_map/ppermute | solution.py:24
  185.9 11.6 %collective-permute-start.27 = (bf16[128,2048]{1,0:T(8,128)(2,1)S(1)}, bf16[128,2048]{1,0:T(8,128)(2,1)S(1)}, u32[]{:S(2)}, u32[]{:S(2)}) collective-permute-start(bf16[128,2048]{1,0:T(8,128)(2,1)S(1)} %fusion.2), channel_id=1, source_target_pairs={{0,3},{1,0},{2,1},{3,2},{4,7},{5,4},{6,5},{7,6},{8,11},{9,8},{10,9... | collective-permute-start | bytes 1572872 | tf_op jit(solution)/shard_map/ppermute | solution.py:24
  185.9 34.3 %collective-permute-start.26 = (bf16[128,2048]{1,0:T(8,128)(2,1)S(1)}, bf16[128,2048]{1,0:T(8,128)(2,1)S(1)}, u32[]{:S(2)}, u32[]{:S(2)}) collective-permute-start(bf16[128,2048]{1,0:T(8,128)(2,1)S(1)} %fusion.2), channel_id=1, source_target_pairs={{0,2},{1,3},{2,0},{3,1},{4,6},{5,7},{6,4},{7,5},{8,10},{9,11},{10,... | collective-permute-start | bytes 1572872 | tf_op jit(solution)/shard_map/ppermute | solution.py:24
  187.0 44.5 %collective-permute-start.25 = (bf16[128,2048]{1,0:T(8,128)(2,1)S(1)}, bf16[128,2048]{1,0:T(8,128)(2,1)S(1)}, u32[]{:S(2)}, u32[]{:S(2)}) collective-permute-start(bf16[128,2048]{1,0:T(8,128)(2,1)S(1)} %fusion.2), channel_id=1, source_target_pairs={{0,1},{1,2},{2,3},{3,0},{4,5},{5,6},{6,7},{7,4},{8,9},{9,10},{10,1... | collective-permute-start | bytes 1572872 | tf_op jit(solution)/shard_map/ppermute | solution.py:24
  241.5 13.3 %collective-permute-start.29 = (bf16[4,32,2048]{2,1,0:T(8,128)(2,1)}, bf16[4,32,2048]{2,1,0:T(8,128)(2,1)}, u32[]{:S(2)}, u32[]{:S(2)}) collective-permute-start(bf16[4,32,2048]{2,1,0:T(8,128)(2,1)} %fusion.3), channel_id=1, source_target_pairs={{0,8},{4,12},{8,0},{12,4},{1,9},{5,13},{9,1},{13,5},{2,10},{6,14},... | collective-permute-start | bytes 1572872 | tf_op jit(solution)/shard_map/ppermute | solution.py:24
  265.9 10.7 %collective-permute-start.33 = (bf16[128,544]{1,0:T(8,128)(2,1)S(1)}, bf16[128,544]{1,0:T(8,128)(2,1)S(1)}, u32[]{:S(2)}, u32[]{:S(2)}) collective-permute-start(bf16[128,544]{1,0:T(8,128)(2,1)S(1)} %get-tuple-element.28), channel_id=1, source_target_pairs={{0,2},{1,3},{2,0},{3,1},{4,6},{5,7},{6,4},{7,5},{8,10},{9,11},{10,... | collective-permute-start | bytes 417800 | tf_op jit(solution)/shard_map/ppermute | solution.py:24
  265.9 14.2 %collective-permute-start.32 = (bf16[128,544]{1,0:T(8,128)(2,1)S(1)}, bf16[128,544]{1,0:T(8,128)(2,1)S(1)}, u32[]{:S(2)}, u32[]{:S(2)}) collective-permute-start(bf16[128,544]{1,0:T(8,128)(2,1)S(1)} %get-tuple-element.28), channel_id=1, source_target_pairs={{0,1},{1,2},{2,3},{3,0},{4,5},{5,6},{6,7},{7,4},{8,9},{9,10},{10,1... | collective-permute-start | bytes 417800 | tf_op jit(solution)/shard_map/ppermute | solution.py:24
  267.2 42.5 %collective-permute-start.39 = (bf16[128,2048]{1,0:T(8,128)(2,1)S(1)}, bf16[128,2048]{1,0:T(8,128)(2,1)S(1)}, u32[]{:S(2)}, u32[]{:S(2)}) collective-permute-start(bf16[128,2048]{1,0:T(8,128)(2,1)S(1)} %finish_mixer.2), channel_id=1, source_target_pairs={{16,0},{17,1},{18,2},{19,3},{20,4},{21,5},{22,6},{23,7},{24,8},{25... | collective-permute-start | bytes 1572872 | tf_op jit(solution)/shard_map/ppermute | solution.py:333
  307.5 13.6 %collective-permute-start.38 = (bf16[128,2048]{1,0:T(8,128)(2,1)S(1)}, bf16[128,2048]{1,0:T(8,128)(2,1)S(1)}, u32[]{:S(2)}, u32[]{:S(2)}) collective-permute-start(bf16[128,2048]{1,0:T(8,128)(2,1)S(1)} %finish_mixer.3), channel_id=1, source_target_pairs={{0,16},{1,17},{2,18},{3,19},{4,20},{5,21},{6,22},{7,23},{8,24},{9,... | collective-permute-start | bytes 1572872 | tf_op jit(solution)/shard_map/ppermute | solution.py:397
  (33 other events, 323.4 us)
